TPU v7x, 128 devices: a whole 4x4x4 slice. The times are simulated.
128 devices in a mesh: row: 16 (over z_hi, x, core), col: 8 (over y, z_lo).
Axes of the slice: x: 4, y: 4, z: 4 (z_hi: 2, z_lo: 2; z = z_hi * 2 + z_lo), core: 2. Of those that a mesh axis runs over, the one named last changes fastest.
Arguments:
- tokens: bfloat16 [2, 4096, 2048], P(None, 'row', 'col'), may hold values from -6 to 6
- out_grad: bfloat16 [2, 4096, 2048], P(None, 'row', 'col'), may hold values from -6 to 6
- parents: int32 [2, 13], replicated, may hold values from 0 to 11, as said below
- routes: int32 [2, 4096, 6], P(None, 'row'), may hold values from 0 to 7, all different within a row; in each aligned block of 256 rows (0 to 255, 256 to 511, ..., all dimensions but the last counted through in order) at most 256 rows name the same one
- gates: float32 [2, 4096, 6], P(None, 'row'), may hold values from 0.2 to 1
- norm_in: bfloat16 [2048], replicated, may hold values from 0.5 to 1.5
- w_query: bfloat16 [2048, 3072], P('row', 'col'), may hold values from -0.125 to 0.125
- w_latent: bfloat16 [2048, 576], P('row', 'col'), may hold values from -0.125 to 0.125
- norm_latent: bfloat16 [512], replicated, may hold values from 0.5 to 1.5
- w_expand: bfloat16 [512, 4096], P('row', 'col'), may hold values from -0.25 to 0.25
- w_output: bfloat16 [2048, 2048], P('col', 'row'), may hold values from -4 to 4
- norm_mid: bfloat16 [2048], replicated, may hold values from 0.5 to 1.5
- w_shared_gate: bfloat16 [2048, 2816], P('row', 'col'), may hold values from -0.125 to 0.125
- w_shared_up: bfloat16 [2048, 2816], P('row', 'col'), may hold values from -0.125 to 0.125
- w_shared_down: bfloat16 [2816, 2048], P('col', 'row'), may hold values from -0.109375 to 0.109375
- w_expert_gate: bfloat16 [8, 2048, 1408], P(None, 'row', 'col'), may hold values from -0.125 to 0.125
- w_expert_up: bfloat16 [8, 2048, 1408], P(None, 'row', 'col'), may hold values from -0.125 to 0.125
- w_expert_down: bfloat16 [8, 1408, 2048], P(None, 'col', 'row'), may hold values from -0.15625 to 0.15625
Outputs:
- layer_out: bfloat16 [2, 4096, 2048], P(None, 'row', 'col')
- input_grad: bfloat16 [2, 4096, 2048], P(None, 'row', 'col')
- grad_norm_in: float32 [2048], replicated
- grad_query: float32 [2048, 3072], P('row', 'col')
- grad_latent: float32 [2048, 576], P('row', 'col')
- grad_norm_latent: float32 [512], replicated
- grad_expand: float32 [512, 4096], P('row', 'col')
- grad_output: float32 [2048, 2048], P('col', 'row')
- grad_norm_mid: float32 [2048], replicated
- grad_shared_gate: float32 [2048, 2816], P('row', 'col')
- grad_shared_up: float32 [2048, 2816], P('row', 'col')
- grad_shared_down: float32 [2816, 2048], P('col', 'row')
- grad_expert_gate: float32 [8, 2048, 1408], P(None, 'row', 'col')
- grad_expert_up: float32 [8, 2048, 1408], P(None, 'row', 'col')
- grad_expert_down: float32 [8, 1408, 2048], P(None, 'col', 'row')
Inputs may be any that keep to these rules, and one draw needn't show every extreme that they name: parents[m, 0] is 0 for the trunk, segment 0, which holds tokens 0 to 1023; segment s >= 1 holds the 256 tokens from 1024 + (s - 1) * 256 on, and parents[m, s] is a segment below s; the last segment's parent is segment 13 - 2. `routes`: each row names 6 different experts; of the 256 tokens of a tree held by one index of row (aligned blocks of 256 rows), no expert is named by more than 256.
All inputs are finite; a program needn't handle non-finite values.
Results may differ from a plain program's by a relative error of at most 0.028.
Values may be sent and summed in bfloat16 or wider, within the bound.
No kernel may reach another device: no remote copies, remote signals or barrier semaphores. Data moves between devices by JAX's collectives and lax.ppermute only.
A program may use at most 320 MiB of HBM per device.

v0:
```python
import jax
import jax.numpy as jnp
from jax import lax
from jax.sharding import PartitionSpec as P

D = 2048
NOPE = 128
ROPE = 64
VDIM = 128
KVL = 512
TOPK = 6
EXPERTS = 8
TRUNK = 1024
BRANCH = 256


EPS = 1e-06
THETA = 10000.0
HIGHEST = lax.Precision.HIGHEST
NEG_LARGE = -1e30


def rounded(values):
    return lax.optimization_barrier(values.astype(jnp.bfloat16)).astype(jnp.float32)


def inverse_rms(values):
    return lax.rsqrt(jnp.mean(values * values, axis=-1, keepdims=True) + EPS)


def norm_backward(grad_out, values, inv_scale, norm_gain):
    weighted = grad_out * norm_gain
    inner = jnp.mean(weighted * values, axis=-1, keepdims=True)
    return inv_scale * weighted - values * (inv_scale * inv_scale * inv_scale) * inner


def rope_tables(positions, width):
    half_width = width // 2
    frequency = THETA ** (-jnp.arange(half_width, dtype=jnp.float32) / half_width)
    angles = positions[:, None] * frequency[None, :]
    return (jnp.cos(angles), jnp.sin(angles))


def rotate(values, cos_table, sin_table):
    half_width = values.shape[-1] // 2
    first_half = values[..., :half_width]
    second_half = values[..., half_width:]
    return jnp.concatenate(
        [
            first_half * cos_table - second_half * sin_table,
            first_half * sin_table + second_half * cos_table,
        ],
        axis=-1,
    )


def unrotate(grads, cos_table, sin_table):
    half_width = grads.shape[-1] // 2
    first_half = grads[..., :half_width]
    second_half = grads[..., half_width:]
    return jnp.concatenate(
        [
            first_half * cos_table + second_half * sin_table,
            second_half * cos_table - first_half * sin_table,
        ],
        axis=-1,
    )


def tree_layout(parent_ids, trunk_len, branch_len, total_len):
    seg_count = parent_ids.shape[0]
    tokens_at = jnp.arange(total_len, dtype=jnp.int32)
    in_trunk = tokens_at < trunk_len
    segment_of = jnp.where(in_trunk, 0, 1 + (tokens_at - trunk_len) // branch_len)
    offset_in = jnp.where(in_trunk, tokens_at, (tokens_at - trunk_len) % branch_len)
    identity = jnp.eye(seg_count, dtype=jnp.float32)
    seg_range = jnp.arange(seg_count, dtype=jnp.int32)
    parent_onehot = (parent_ids[:, None] == seg_range[None, :]).astype(jnp.float32)
    ancestry = identity
    for repeat in range(seg_count - 1):
        ancestry = jnp.maximum(identity, jnp.dot(parent_onehot, ancestry, precision=HIGHEST))
    seg_lengths = jnp.where(seg_range == 0, trunk_len, branch_len).astype(jnp.float32)
    starts = jnp.dot(ancestry - identity, seg_lengths, precision=HIGHEST)
    member = (segment_of[:, None] == seg_range[None, :]).astype(jnp.float32)
    positions = jnp.dot(member, starts, precision=HIGHEST) + offset_in.astype(jnp.float32)
    return (member, positions, ancestry)


def visibility(member, ancestry, query_start, query_count):
    total_len = member.shape[0]
    query_member = lax.dynamic_slice_in_dim(member, query_start, query_count, 0)
    reach_seg = jnp.dot(query_member, ancestry, precision=HIGHEST)
    reachable = jnp.einsum("qs,ks->qk", reach_seg, member, precision=HIGHEST)
    same_seg = jnp.einsum("qs,ks->qk", query_member, member, precision=HIGHEST)
    query_ids = query_start + jnp.arange(query_count, dtype=jnp.int32)
    key_ids = jnp.arange(total_len, dtype=jnp.int32)
    causal = key_ids[None, :] <= query_ids[:, None]
    return (reachable > 0.5) & ((same_seg < 0.5) | causal)


def dispatch_tables(route_ids, gate_values, expert_count, capacity):
    token_count, top_count = route_ids.shape
    flat_routes = route_ids.reshape(-1)
    onehot = (flat_routes[:, None] == jnp.arange(expert_count, dtype=jnp.int32)[None, :]).astype(
        jnp.int32
    )
    before = jnp.cumsum(onehot, axis=0) - onehot
    slot_of = jnp.sum(before * onehot, axis=1)
    owner_row = jnp.arange(token_count * top_count, dtype=jnp.int32) // top_count
    slot_token = (
        jnp.full((expert_count, capacity), token_count, jnp.int32)
        .at[flat_routes, slot_of]
        .set(owner_row)
    )
    slot_gate = (
        jnp.zeros((expert_count, capacity), jnp.float32)
        .at[flat_routes, slot_of]
        .set(gate_values.reshape(-1))
    )
    return (slot_token, slot_gate)


def silu_parts(gate_pre):
    sig_value = jax.nn.sigmoid(gate_pre)
    return (gate_pre * sig_value, sig_value * (1.0 + gate_pre * (1.0 - sig_value)))


def fetch_attention(w_query, w_latent, w_expand, w_output):
    return (
        lax.all_gather(w_query, "row", axis=0, tiled=True),
        lax.all_gather(w_latent, "row", axis=0, tiled=True),
        lax.all_gather(w_expand, "row", axis=0, tiled=True),
        lax.all_gather(w_output, "row", axis=1, tiled=True),
    )


def fetch_feedforward(
    w_shared_gate, w_shared_up, w_shared_down, w_expert_gate, w_expert_up, w_expert_down
):
    return (
        lax.all_gather(w_shared_gate, "row", axis=0, tiled=True),
        lax.all_gather(w_shared_up, "row", axis=0, tiled=True),
        lax.all_gather(w_shared_down, "row", axis=1, tiled=True),
        lax.all_gather(w_expert_gate, "row", axis=1, tiled=True),
        lax.all_gather(w_expert_up, "row", axis=1, tiled=True),
        lax.all_gather(w_expert_down, "row", axis=2, tiled=True),
    )


def reduce_grads(grads):
    return (
        lax.psum_scatter(
            grads[0].astype(jnp.bfloat16), "row", scatter_dimension=0, tiled=True
        ).astype(jnp.float32),
        lax.psum_scatter(
            grads[1].astype(jnp.bfloat16), "row", scatter_dimension=0, tiled=True
        ).astype(jnp.float32),
        lax.psum_scatter(
            grads[2].astype(jnp.bfloat16), "row", scatter_dimension=0, tiled=True
        ).astype(jnp.float32),
        lax.psum_scatter(
            grads[3].astype(jnp.bfloat16), "row", scatter_dimension=1, tiled=True
        ).astype(jnp.float32),
        lax.psum_scatter(
            grads[4].astype(jnp.bfloat16), "row", scatter_dimension=0, tiled=True
        ).astype(jnp.float32),
        lax.psum_scatter(
            grads[5].astype(jnp.bfloat16), "row", scatter_dimension=0, tiled=True
        ).astype(jnp.float32),
        lax.psum_scatter(
            grads[6].astype(jnp.bfloat16), "row", scatter_dimension=1, tiled=True
        ).astype(jnp.float32),
        lax.psum_scatter(
            grads[7].astype(jnp.bfloat16), "row", scatter_dimension=1, tiled=True
        ).astype(jnp.float32),
        lax.psum_scatter(
            grads[8].astype(jnp.bfloat16), "row", scatter_dimension=1, tiled=True
        ).astype(jnp.float32),
        lax.psum_scatter(
            grads[9].astype(jnp.bfloat16), "row", scatter_dimension=2, tiled=True
        ).astype(jnp.float32),
    )


def local(
    tokens,
    out_grad,
    parents,
    routes,
    gates,
    norm_in,
    w_query,
    w_latent,
    norm_latent,
    w_expand,
    w_output,
    norm_mid,
    w_shared_gate,
    w_shared_up,
    w_shared_down,
    w_expert_gate,
    w_expert_up,
    w_expert_down,
):
    micro_count, local_rows, local_width = tokens.shape
    row_rank = lax.axis_index("row")
    col_rank = lax.axis_index("col")
    tree_len = local_rows * lax.axis_size("row")
    latent_cols = w_latent.shape[1]
    heads_here = w_query.shape[1] // (NOPE + ROPE)
    capacity = local_rows * TOPK * 4 // (3 * EXPERTS)
    score_scale = (NOPE + ROPE) ** (-0.5)
    query_start = row_rank * local_rows
    gain_in = norm_in.astype(jnp.float32)
    gain_latent = norm_latent.astype(jnp.float32)
    gain_mid = norm_mid.astype(jnp.float32)
    outputs = []
    input_grads = []
    for micro_index in range(micro_count):
        query_full, latent_full, expand_full, output_full = fetch_attention(
            w_query, w_latent, w_expand, w_output
        )
        (
            shared_gate_full,
            shared_up_full,
            shared_down_full,
            expert_gate_full,
            expert_up_full,
            expert_down_full,
        ) = fetch_feedforward(
            w_shared_gate, w_shared_up, w_shared_down, w_expert_gate, w_expert_up, w_expert_down
        )
        inputs_full = lax.all_gather(tokens[micro_index], "col", axis=1, tiled=True)
        inputs_float = inputs_full.astype(jnp.float32)
        scale_in = inverse_rms(inputs_float)
        normed_in = (inputs_float * scale_in * gain_in).astype(jnp.bfloat16)
        member, positions, ancestry = tree_layout(parents[micro_index], TRUNK, BRANCH, tree_len)
        own_positions = lax.dynamic_slice_in_dim(positions, query_start, local_rows, 0)
        cos_table, sin_table = rope_tables(own_positions, ROPE)
        visible = visibility(member, ancestry, query_start, local_rows)
        query_pre = jnp.dot(normed_in, query_full, preferred_element_type=jnp.float32).reshape(
            local_rows, heads_here, NOPE + ROPE
        )
        query_nope = query_pre[..., :NOPE].astype(jnp.bfloat16)
        query_rope = rotate(
            query_pre[..., NOPE:], cos_table[:, None, :], sin_table[:, None, :]
        ).astype(jnp.bfloat16)
        latent_part = jnp.dot(normed_in, latent_full, preferred_element_type=jnp.float32).astype(
            jnp.bfloat16
        )
        latent = lax.all_gather(latent_part, "col", axis=1, tiled=True)
        compressed = latent[:, :KVL].astype(jnp.float32)
        scale_latent = inverse_rms(compressed)
        latent_normed = (compressed * scale_latent * gain_latent).astype(jnp.bfloat16)
        expanded = jnp.dot(latent_normed, expand_full, preferred_element_type=jnp.float32).astype(
            jnp.bfloat16
        )
        rope_keys = rotate(latent[:, KVL:].astype(jnp.float32), cos_table, sin_table).astype(
            jnp.bfloat16
        )
        key_pack, rope_pack = (
            lax.all_gather(expanded, "row", axis=0, tiled=True),
            lax.all_gather(rope_keys, "row", axis=0, tiled=True),
        )
        key_heads = key_pack.reshape(tree_len, heads_here, NOPE + VDIM)
        key_nope = key_heads[..., :NOPE]
        key_vals = key_heads[..., NOPE:]

        def score_block():
            raw = jnp.einsum(
                "qhd,khd->hqk", query_nope, key_nope, preferred_element_type=jnp.float32
            ) + jnp.einsum("qhr,kr->hqk", query_rope, rope_pack, preferred_element_type=jnp.float32)
            return jnp.where(visible[None], raw * score_scale, NEG_LARGE)

        scores = score_block()
        row_max = jnp.max(scores, axis=-1, keepdims=True)
        log_total = row_max + jnp.log(jnp.sum(jnp.exp(scores - row_max), axis=-1, keepdims=True))
        probs_low = jnp.exp(scores - log_total).astype(jnp.bfloat16)
        attended = (
            jnp.einsum("hqk,khd->qhd", probs_low, key_vals, preferred_element_type=jnp.float32)
            .reshape(local_rows, heads_here * VDIM)
            .astype(jnp.bfloat16)
        )
        attn_part = jnp.dot(attended, output_full, preferred_element_type=jnp.float32)
        attn_full = lax.psum(attn_part.astype(jnp.bfloat16), "col").astype(jnp.float32)
        residual = inputs_float + attn_full
        scale_mid = inverse_rms(residual)
        normed_mid = (residual * scale_mid * gain_mid).astype(jnp.bfloat16)
        shared_gate_pre = jnp.dot(normed_mid, shared_gate_full, preferred_element_type=jnp.float32)
        shared_up_pre = jnp.dot(normed_mid, shared_up_full, preferred_element_type=jnp.float32)
        shared_silu, shared_slope = silu_parts(shared_gate_pre)
        shared_act = (shared_silu * shared_up_pre).astype(jnp.bfloat16)
        shared_part = jnp.dot(shared_act, shared_down_full, preferred_element_type=jnp.float32)
        slot_token, slot_gate = dispatch_tables(
            routes[micro_index], gates[micro_index], EXPERTS, capacity
        )
        padded_mid = jnp.concatenate([normed_mid, jnp.zeros((1, D), jnp.bfloat16)], axis=0)
        buffers = padded_mid[slot_token]
        expert_gate_pre = jnp.einsum(
            "ecd,edf->ecf", buffers, expert_gate_full, preferred_element_type=jnp.float32
        )
        expert_up_pre = jnp.einsum(
            "ecd,edf->ecf", buffers, expert_up_full, preferred_element_type=jnp.float32
        )
        expert_silu, expert_slope = silu_parts(expert_gate_pre)
        expert_act = (expert_silu * expert_up_pre).astype(jnp.bfloat16)
        expert_out = jnp.einsum(
            "ecf,efd->ecd", expert_act, expert_down_full, preferred_element_type=jnp.float32
        )
        routed_part = (
            jnp.zeros((local_rows + 1, D), jnp.float32)
            .at[slot_token]
            .add(expert_out * slot_gate[..., None])[:local_rows]
        )
        ffn_local = lax.psum_scatter(
            (routed_part + shared_part).astype(jnp.bfloat16), "col", scatter_dimension=1, tiled=True
        ).astype(jnp.float32)
        residual_local = lax.dynamic_slice_in_dim(residual, col_rank * local_width, local_width, 1)
        outputs.append((residual_local + ffn_local).astype(jnp.bfloat16))
        grad_full = lax.all_gather(out_grad[micro_index], "col", axis=1, tiled=True)
        grad_float = grad_full.astype(jnp.float32)
        grad_shared_down = jnp.einsum(
            "tf,td->fd", shared_act, grad_full, preferred_element_type=jnp.float32
        )
        d_shared_act = rounded(
            jnp.einsum("td,fd->tf", grad_full, shared_down_full, preferred_element_type=jnp.float32)
        )
        d_shared_gate = (d_shared_act * shared_up_pre * shared_slope).astype(jnp.bfloat16)
        d_shared_up = (d_shared_act * shared_silu).astype(jnp.bfloat16)
        grad_shared_gate = jnp.einsum(
            "td,tf->df", normed_mid, d_shared_gate, preferred_element_type=jnp.float32
        )
        grad_shared_up = jnp.einsum(
            "td,tf->df", normed_mid, d_shared_up, preferred_element_type=jnp.float32
        )
        d_mid = jnp.einsum(
            "tf,df->td", d_shared_gate, shared_gate_full, preferred_element_type=jnp.float32
        ) + jnp.einsum("tf,df->td", d_shared_up, shared_up_full, preferred_element_type=jnp.float32)
        padded_grad = jnp.concatenate([grad_full, jnp.zeros((1, D), jnp.bfloat16)], axis=0)
        d_expert_out = (slot_gate[..., None] * padded_grad[slot_token].astype(jnp.float32)).astype(
            jnp.bfloat16
        )
        grad_expert_down = jnp.einsum(
            "ecf,ecd->efd", expert_act, d_expert_out, preferred_element_type=jnp.float32
        )
        d_expert_act = rounded(
            jnp.einsum(
                "ecd,efd->ecf", d_expert_out, expert_down_full, preferred_element_type=jnp.float32
            )
        )
        d_expert_gate = (d_expert_act * expert_up_pre * expert_slope).astype(jnp.bfloat16)
        d_expert_up = (d_expert_act * expert_silu).astype(jnp.bfloat16)
        grad_expert_gate = jnp.einsum(
            "ecd,ecf->edf", buffers, d_expert_gate, preferred_element_type=jnp.float32
        )
        grad_expert_up = jnp.einsum(
            "ecd,ecf->edf", buffers, d_expert_up, preferred_element_type=jnp.float32
        )
        d_buffers = jnp.einsum(
            "ecf,edf->ecd", d_expert_gate, expert_gate_full, preferred_element_type=jnp.float32
        ) + jnp.einsum(
            "ecf,edf->ecd", d_expert_up, expert_up_full, preferred_element_type=jnp.float32
        )
        d_mid = (
            d_mid
            + jnp.zeros((local_rows + 1, D), jnp.float32).at[slot_token].add(d_buffers)[:local_rows]
        )
        d_mid_full = lax.psum(d_mid.astype(jnp.bfloat16), "col").astype(jnp.float32)
        mid_gain_term = jnp.sum(d_mid_full * residual * scale_mid, axis=0)
        d_residual = grad_float + norm_backward(d_mid_full, residual, scale_mid, gain_mid)
        d_attn_low = d_residual.astype(jnp.bfloat16)
        grad_output = jnp.einsum(
            "to,td->od", attended, d_attn_low, preferred_element_type=jnp.float32
        )
        d_attended = (
            jnp.einsum("td,od->to", d_attn_low, output_full, preferred_element_type=jnp.float32)
            .astype(jnp.bfloat16)
            .reshape(local_rows, heads_here, VDIM)
        )
        scores = score_block()
        attn_probs = jnp.exp(scores - log_total)
        d_probs = jnp.einsum(
            "qhd,khd->hqk", d_attended, key_vals, preferred_element_type=jnp.float32
        )
        d_vals = jnp.einsum(
            "hqk,qhd->khd",
            attn_probs.astype(jnp.bfloat16),
            d_attended,
            preferred_element_type=jnp.float32,
        )
        prob_dot = jnp.sum(d_probs * attn_probs, axis=-1, keepdims=True)
        d_raw = (attn_probs * (d_probs - prob_dot) * score_scale).astype(jnp.bfloat16)
        d_query_nope = jnp.einsum(
            "hqk,khd->qhd", d_raw, key_nope, preferred_element_type=jnp.float32
        )
        d_query_rope = jnp.einsum(
            "hqk,kr->qhr", d_raw, rope_pack, preferred_element_type=jnp.float32
        )
        d_key_nope = jnp.einsum(
            "hqk,qhd->khd", d_raw, query_nope, preferred_element_type=jnp.float32
        )
        d_rope_keys = jnp.einsum(
            "hqk,qhr->kr", d_raw, query_rope, preferred_element_type=jnp.float32
        )
        d_key_pack = jnp.concatenate([d_key_nope, d_vals], axis=-1).reshape(
            tree_len, heads_here * (NOPE + VDIM)
        )
        d_expanded, d_rope_own = (
            lax.psum_scatter(
                d_key_pack.astype(jnp.bfloat16), "row", scatter_dimension=0, tiled=True
            ).astype(jnp.float32),
            lax.psum_scatter(
                d_rope_keys.astype(jnp.bfloat16), "row", scatter_dimension=0, tiled=True
            ).astype(jnp.float32),
        )
        d_expanded_low = d_expanded.astype(jnp.bfloat16)
        grad_expand = jnp.einsum(
            "tk,te->ke", latent_normed, d_expanded_low, preferred_element_type=jnp.float32
        )
        d_latent_normed = jnp.einsum(
            "te,ke->tk", d_expanded_low, expand_full, preferred_element_type=jnp.float32
        )
        d_rope_pre = unrotate(d_rope_own, cos_table, sin_table)
        d_latent_normed, d_rope_pre = (
            lax.psum(d_latent_normed.astype(jnp.bfloat16), "col").astype(jnp.float32),
            lax.psum(d_rope_pre.astype(jnp.bfloat16), "col").astype(jnp.float32),
        )
        latent_gain_term = jnp.sum(d_latent_normed * compressed * scale_latent, axis=0)
        d_compressed = norm_backward(d_latent_normed, compressed, scale_latent, gain_latent)
        d_latent_low = jnp.concatenate([d_compressed, d_rope_pre], axis=1).astype(jnp.bfloat16)
        d_latent_own = lax.dynamic_slice_in_dim(
            d_latent_low, col_rank * latent_cols, latent_cols, 1
        )
        grad_latent = jnp.einsum(
            "td,tl->dl", normed_in, d_latent_own, preferred_element_type=jnp.float32
        )
        d_query_pre = (
            jnp.concatenate(
                [
                    d_query_nope,
                    unrotate(d_query_rope, cos_table[:, None, :], sin_table[:, None, :]),
                ],
                axis=-1,
            )
            .reshape(local_rows, heads_here * (NOPE + ROPE))
            .astype(jnp.bfloat16)
        )
        grad_query = jnp.einsum(
            "td,tq->dq", normed_in, d_query_pre, preferred_element_type=jnp.float32
        )
        d_normed_in = jnp.einsum(
            "tq,dq->td", d_query_pre, query_full, preferred_element_type=jnp.float32
        ) + jnp.einsum("tl,dl->td", d_latent_own, latent_full, preferred_element_type=jnp.float32)
        d_in_full = lax.psum(d_normed_in.astype(jnp.bfloat16), "col").astype(jnp.float32)
        in_gain_term = jnp.sum(d_in_full * inputs_float * scale_in, axis=0)
        d_tokens = d_residual + norm_backward(d_in_full, inputs_float, scale_in, gain_in)
        input_grads.append(
            lax.dynamic_slice_in_dim(d_tokens, col_rank * local_width, local_width, 1).astype(
                jnp.bfloat16
            )
        )
        step_grads = (
            grad_query,
            grad_latent,
            grad_expand,
            grad_output,
            grad_shared_gate,
            grad_shared_up,
            grad_shared_down,
            grad_expert_gate,
            grad_expert_up,
            grad_expert_down,
        )
        gathered_sum = (
            step_grads if micro_index == 0 else jax.tree.map(jnp.add, gathered_sum, step_grads)
        )
        in_gain_sum = in_gain_term if micro_index == 0 else in_gain_sum + in_gain_term
        latent_gain_sum = (
            latent_gain_term if micro_index == 0 else latent_gain_sum + latent_gain_term
        )
        mid_gain_sum = mid_gain_term if micro_index == 0 else mid_gain_sum + mid_gain_term
    scattered_sum = reduce_grads(gathered_sum)
    gain_totals = lax.psum((in_gain_sum, latent_gain_sum, mid_gain_sum), "row")
    return (
        jnp.stack(outputs),
        jnp.stack(input_grads),
        gain_totals[0],
        scattered_sum[0],
        scattered_sum[1],
        gain_totals[1],
        scattered_sum[2],
        scattered_sum[3],
        gain_totals[2],
        scattered_sum[4],
        scattered_sum[5],
        scattered_sum[6],
        scattered_sum[7],
        scattered_sum[8],
        scattered_sum[9],
    )


def solution(mesh):
    in_specs = (
        P(None, "row", "col"),
        P(None, "row", "col"),
        P(),
        P(None, "row", None),
        P(None, "row", None),
        P(),
        P("row", "col"),
        P("row", "col"),
        P(),
        P("row", "col"),
        P("col", "row"),
        P(),
        P("row", "col"),
        P("row", "col"),
        P("col", "row"),
        P(None, "row", "col"),
        P(None, "row", "col"),
        P(None, "col", "row"),
    )
    out_specs = (
        P(None, "row", "col"),
        P(None, "row", "col"),
        P(),
        P("row", "col"),
        P("row", "col"),
        P(),
        P("row", "col"),
        P("col", "row"),
        P(),
        P("row", "col"),
        P("row", "col"),
        P("col", "row"),
        P(None, "row", "col"),
        P(None, "row", "col"),
        P(None, "col", "row"),
    )
    return jax.shard_map(local, mesh=mesh, in_specs=in_specs, out_specs=out_specs, check_vma=False)
```

profile of v0, /device:TPU:0, one launch (start us, length us, event | category | flops | bytes accessed | tf_op | source)
XLA Modules:
  0.0 2545.0 jit_solution(10711721784636388295)
XLA Ops:
  63.6 28.9 %all_gather.72 = bf16[256,576]{0,1:T(8,128)(2,1)S(1)} all-gather(bf16[256,72]{0,1:T(8,128)(2,1)S(1)} %convolution_convert_fusion.17), channel_id=1, replica_groups=mesh['row'=16,'col'=8] {'col'}, dimensions={1}, use_global_device_ids=true | all-gather | bytes 331776 | tf_op jit(solution)/shard_map/all_gather | solution.py:251
  228.5 41.9 %all-gather.37.cloned.1.call-done = bf16[4096,512]{1,0:T(8,128)(2,1)} async-done(((bf16[256,512]{1,0:T(8,128)(2,1)}), bf16[4096,512]{1,0:T(8,128)(2,1)}) %all-gather.37.cloned.1.call-update) | async-done | bytes 4194320 | tf_op jit(solution)/shard_map/all_gather | solution.py:262
  363.9 40.8 %all-gather.45.cloned.1.call-done = bf16[1,256,2048]{2,1,0:T(8,128)(2,1)} async-done(((bf16[1,256,256]{2,1,0:T(8,128)(2,1)}), bf16[1,256,2048]{2,1,0:T(8,128)(2,1)}) %all-gather.45.cloned.1.call-update) | async-done | bytes 1048592 | tf_op jit(solution)/shard_map/all_gather | solution.py:320
  428.3 29.4 %all-gather.35.cloned.1.call-done = bf16[352,2048]{1,0:T(8,128)(2,1)} async-done(((bf16[352,128]{1,0:T(8,128)(2,1)}), bf16[352,2048]{1,0:T(8,128)(2,1)}) %all-gather.35.cloned.1.call-update) | async-done | bytes 1441808 | tf_op jit(solution)/shard_map/all_gather | solution.py:143
  463.2 62.1 %all-gather.29.cloned.1.call-done = bf16[8,176,2048]{2,1,0:T(8,128)(2,1)} async-done(((bf16[8,176,128]{2,1,0:T(8,128)(2,1)}), bf16[8,176,2048]{2,1,0:T(8,128)(2,1)}) %all-gather.29.cloned.1.call-update) | async-done | bytes 5767184 | tf_op jit(solution)/shard_map/all_gather | solution.py:146
  542.0 89.3 %all-reduce.24.cloned.1.call-done = (bf16[256,2048]{1,0:T(8,128)(2,1)}, bf16[256,2048]{1,0:T(8,128)(2,1)}) async-done(((bf16[256,2048]{1,0:T(8,128)(2,1)}, bf16[256,2048]{1,0:T(8,128)(2,1)}), (bf16[256,2048]{1,0:T(8,128)(2,1)}, bf16[256,2048]{1,0:T(8,128)(2,1)})) %all-reduce.24.cloned.1.call-update) | async-done | bytes 2097168 | tf_op jit(solution)/shard_map/psum | solution.py:285
  660.6 39.9 %all-gather.25.cloned.1.call-done = bf16[8,2048,176]{1,2,0:T(8,128)(2,1)} async-done(((bf16[8,128,176]{1,2,0:T(8,128)(2,1)}), bf16[8,2048,176]{1,2,0:T(8,128)(2,1)}) %all-gather.25.cloned.1.call-update) | async-done | bytes 5767184 | tf_op jit(solution)/shard_map/all_gather | solution.py:144
  716.0 52.0 %all-gather.27.cloned.1.call-done = bf16[8,2048,176]{1,2,0:T(8,128)(2,1)} async-done(((bf16[8,128,176]{1,2,0:T(8,128)(2,1)}), bf16[8,2048,176]{1,2,0:T(8,128)(2,1)}) %all-gather.27.cloned.1.call-update) | async-done | bytes 5767184 | tf_op jit(solution)/shard_map/all_gather | solution.py:145
  814.1 28.8 %scatter_custom_fusion.2 = f32[257,2048]{1,0:T(8,128)} fusion(s32[2048]{0:T(1024)S(1)} %bitcast.390, f32[2048,2048]{1,0:T(8,128)} %bitcast.355, f32[]{:T(128)} %constant.92.clone.1), kind=kCustom, calls=%fused_computation.219 | custom fusion | flops 4194304 | bytes 2105856 | tf_op jit(solution)/shard_map/scatter-add | solution.py:366
  870.2 29.0 %scatter_custom_fusion.3 = f32[257,2048]{1,0:T(8,128)} fusion(s32[2048]{0:T(1024)} %bitcast.387, f32[2048,2048]{1,0:T(8,128)} %bitcast.356, f32[]{:T(128)} %constant.92.clone.1), kind=kCustom, calls=%fused_computation.217 | custom fusion | flops 4194304 | bytes 2105856 | tf_op jit(solution)/shard_map/scatter-add | solution.py:366
  914.0 103.7 %all-reduce.22.cloned.1.call-done = (bf16[256,2048]{1,0:T(8,128)(2,1)}, bf16[256,2048]{1,0:T(8,128)(2,1)}) async-done(((bf16[256,2048]{1,0:T(8,128)(2,1)}, bf16[256,2048]{1,0:T(8,128)(2,1)}), (bf16[256,2048]{1,0:T(8,128)(2,1)}, bf16[256,2048]{1,0:T(8,128)(2,1)})) %all-reduce.22.cloned.1.call-update) | async-done | bytes 2097168 | tf_op jit(solution)/shard_map/psum | solution.py:368
  1141.0 81.3 %reduce-scatter.41.cloned.1.call-done = bf16[256,512]{0,1:T(8,128)(2,1)} async-done(((bf16[4096,512]{0,1:T(8,128)(2,1)}), bf16[256,512]{0,1:T(8,128)(2,1)}) %reduce-scatter.41.cloned.1.call-update) | async-done | bytes 262160 | tf_op jit(solution)/shard_map/reduce_scatter | solution.py:409
  1290.7 67.8 %reduce-scatter.39.cloned.1.call-done = bf16[256,64]{0,1:T(8,128)(2,1)} async-done(((bf16[4096,64]{0,1:T(8,128)(2,1)}), bf16[256,64]{0,1:T(8,128)(2,1)}) %reduce-scatter.39.cloned.1.call-update) | async-done | bytes 32784 | tf_op jit(solution)/shard_map/reduce_scatter | solution.py:412
  1665.9 69.8 %reduce-scatter.55.cloned.1.call-done = bf16[128,352]{1,0:T(8,128)(2,1)} async-done(((bf16[2048,352]{1,0:T(8,128)(2,1)}), bf16[128,352]{1,0:T(8,128)(2,1)}) %reduce-scatter.55.cloned.1.call-update) | async-done | bytes 90128
  1737.4 69.8 %reduce-scatter.57.cloned.1.call-done = bf16[128,352]{1,0:T(8,128)(2,1)} async-done(((bf16[2048,352]{1,0:T(8,128)(2,1)}), bf16[128,352]{1,0:T(8,128)(2,1)}) %reduce-scatter.57.cloned.1.call-update) | async-done | bytes 90128
  1808.9 67.8 %reduce-scatter.51.cloned.1.call-done = bf16[128,256]{1,0:T(8,128)(2,1)} async-done(((bf16[2048,256]{1,0:T(8,128)(2,1)}), bf16[128,256]{1,0:T(8,128)(2,1)}) %reduce-scatter.51.cloned.1.call-update) | async-done | bytes 65552
  1878.4 70.6 %reduce-scatter.45.cloned.1.call-done = bf16[128,384]{1,0:T(8,128)(2,1)} async-done(((bf16[2048,384]{1,0:T(8,128)(2,1)}), bf16[128,384]{1,0:T(8,128)(2,1)}) %reduce-scatter.45.cloned.1.call-update) | async-done | bytes 98320 | tf_op jit(solution)/shard_map/reduce_scatter | solution.py:152
  1950.6 89.0 %reduce-scatter.61.cloned.1.call-done = bf16[128,1408]{1,0:T(8,128)(2,1)} async-done(((bf16[2048,1408]{1,0:T(8,128)(2,1)}), bf16[128,1408]{1,0:T(8,128)(2,1)}) %reduce-scatter.61.cloned.1.call-update) | async-done | bytes 360464
  2042.6 87.3 %reduce-scatter.59.cloned.1.call-done = bf16[128,1408]{1,0:T(8,128)(2,1)} async-done(((bf16[2048,1408]{1,0:T(8,128)(2,1)}), bf16[128,1408]{1,0:T(8,128)(2,1)}) %reduce-scatter.59.cloned.1.call-update) | async-done | bytes 360464
  2133.0 87.3 %reduce-scatter.63.cloned.1.call-done = bf16[128,1408]{1,0:T(8,128)(2,1)} async-done(((bf16[2048,1408]{1,0:T(8,128)(2,1)}), bf16[128,1408]{1,0:T(8,128)(2,1)}) %reduce-scatter.63.cloned.1.call-update) | async-done | bytes 360464
  2223.3 64.9 %reduce-scatter.47.cloned.1.call-done = bf16[32,512]{1,0:T(8,128)(2,1)} async-done(((bf16[512,512]{1,0:T(8,128)(2,1)}), bf16[32,512]{1,0:T(8,128)(2,1)}) %reduce-scatter.47.cloned.1.call-update) | async-done | bytes 32784 | tf_op jit(solution)/shard_map/reduce_scatter | solution.py:158
  2289.7 66.8 %reduce-scatter.49.cloned.1.call-done = bf16[128,72]{1,0:T(8,128)(2,1)} async-done(((bf16[2048,72]{1,0:T(8,128)(2,1)}), bf16[128,72]{1,0:T(8,128)(2,1)}) %reduce-scatter.49.cloned.1.call-update) | async-done | bytes 18448
  2357.9 105.4 %all-reduce.18.cloned.1.call-done = (bf16[256,2048]{1,0:T(8,128)(2,1)}, bf16[256,2048]{1,0:T(8,128)(2,1)}) async-done(((bf16[256,2048]{1,0:T(8,128)(2,1)}, bf16[256,2048]{1,0:T(8,128)(2,1)}), (bf16[256,2048]{1,0:T(8,128)(2,1)}, bf16[256,2048]{1,0:T(8,128)(2,1)})) %all-reduce.18.cloned.1.call-update) | async-done | bytes 2097168 | tf_op jit(solution)/shard_map/psum | solution.py:454
  2469.6 68.6 %all-reduce.4 = (f32[2048]{0:T(1024)}, f32[512]{0:T(512)}, f32[2048]{0:T(1024)}) all-reduce(f32[2048]{0:T(1024)S(1)} %add.493, f32[512]{0:T(512)S(1)} %add.496, f32[2048]{0:T(1024)S(1)} %add.499), channel_id=1, replica_groups=mesh['row'=16,'col'=8] {'row'}, use_global_device_ids=true, to_apply=%region_50.51 | all-reduce | flops 4608 | bytes 36864 | tf_op jit(solution)/shard_map/psum | solution.py:483
  (642 shorter events, 986.0 us)
Async XLA Ops:
  139.5 265.2 %all-gather.45.cloned.1.call-start = ((), (), s32[]{:S(2)}) async-start(), calls=%async_computation.37 | async-start | bytes 1179648 | tf_op jit(solution)/shard_map/all_gather | solution.py:320
  140.2 317.4 %all-gather.35.cloned.1.call-start = ((), (), s32[]{:S(2)}) async-start(), calls=%async_computation.24 | async-start | bytes 1531904 | tf_op jit(solution)/shard_map/all_gather | solution.py:143
  141.0 384.4 %all-gather.29.cloned.1.call-start = ((), (), s32[]{:S(2)}) async-start(), calls=%async_computation.21 | async-start | bytes 6127616 | tf_op jit(solution)/shard_map/all_gather | solution.py:146
  141.6 489.7 %all-reduce.24.cloned.1.call-start = ((), (), s32[]{:S(2)}) async-start(), calls=%async_computation.50 | async-start | bytes 4194304 | tf_op jit(solution)/shard_map/psum | solution.py:285
  326.9 373.5 %all-gather.25.cloned.1.call-start = ((), (), s32[]{:S(2)}) async-start(), calls=%async_computation.19 | async-start | bytes 6127616 | tf_op jit(solution)/shard_map/all_gather | solution.py:144
  327.5 440.6 %all-gather.27.cloned.1.call-start = ((), (), s32[]{:S(2)}) async-start(), calls=%async_computation.20 | async-start | bytes 6127616 | tf_op jit(solution)/shard_map/all_gather | solution.py:145
  328.3 571.0 %all-gather.31.cloned.1.call-start = ((), (), s32[]{:S(2)}) async-start(), calls=%async_computation.22 | async-start | bytes 1531904 | tf_op jit(solution)/shard_map/all_gather | solution.py:141
  328.8 575.8 %all-gather.33.cloned.1.call-start = ((), (), s32[]{:S(2)}) async-start(), calls=%async_computation.23 | async-start | bytes 1531904 | tf_op jit(solution)/shard_map/all_gather | solution.py:142
  329.4 688.3 %all-reduce.22.cloned.1.call-start = ((), (), s32[]{:S(2)}) async-start(), calls=%async_computation.49 | async-start | bytes 4194304 | tf_op jit(solution)/shard_map/psum | solution.py:368
  1123.1 517.7 %all-reduce.20.cloned.1.call-start = ((), (), s32[]{:S(2)}) async-start(), calls=%async_computation.48 | async-start | bytes 1048576 | tf_op jit(solution)/shard_map/psum | solution.py:425
  1224.4 419.4 %all-reduce.16.cloned.1.call-start = ((), (), s32[]{:S(2)}) async-start(), calls=%async_computation.46 | async-start | bytes 131072 | tf_op jit(solution)/shard_map/psum | solution.py:426
  1360.8 293.3 %reduce-scatter.33.cloned.1.call-start = ((), (), s32[]{:S(2)}) async-start(), calls=%async_computation.25 | async-start | bytes 1179648 | tf_op jit(solution)/shard_map/reduce_scatter | solution.py:315
  1364.6 290.5 %reduce-scatter.35.cloned.1.call-start = ((), (), s32[]{:S(2)}) async-start(), calls=%async_computation.27 | async-start | bytes 1179648 | tf_op jit(solution)/shard_map/reduce_scatter | solution.py:315
  1408.9 255.2 %reduce-scatter.53.cloned.1.call-start = ((), (), s32[]{:S(2)}) async-start(), calls=%async_computation.40 | async-start | bytes 1671168
  1415.7 320.0 %reduce-scatter.55.cloned.1.call-start = ((), (), s32[]{:S(2)}) async-start(), calls=%async_computation.41 | async-start | bytes 1671168
  1423.2 384.0 %reduce-scatter.57.cloned.1.call-start = ((), (), s32[]{:S(2)}) async-start(), calls=%async_computation.42 | async-start | bytes 1671168
  1428.8 447.9 %reduce-scatter.51.cloned.1.call-start = ((), (), s32[]{:S(2)}) async-start(), calls=%async_computation.39 | async-start | bytes 1114112
  1464.1 484.9 %reduce-scatter.45.cloned.1.call-start = ((), (), s32[]{:S(2)}) async-start(), calls=%async_computation.32 | async-start | bytes 1671168 | tf_op jit(solution)/shard_map/reduce_scatter | solution.py:152
  1499.0 540.6 %reduce-scatter.61.cloned.1.call-start = ((), (), s32[]{:S(2)}) async-start(), calls=%async_computation.44 | async-start | bytes 6127616
  1541.0 588.9 %reduce-scatter.59.cloned.1.call-start = ((), (), s32[]{:S(2)}) async-start(), calls=%async_computation.43 | async-start | bytes 6127616
  1582.3 638.0 %reduce-scatter.63.cloned.1.call-start = ((), (), s32[]{:S(2)}) async-start(), calls=%async_computation.45 | async-start | bytes 6127616
  1631.9 656.4 %reduce-scatter.47.cloned.1.call-start = ((), (), s32[]{:S(2)}) async-start(), calls=%async_computation.33 | async-start | bytes 557056 | tf_op jit(solution)/shard_map/reduce_scatter | solution.py:158
  1640.7 715.8 %reduce-scatter.49.cloned.1.call-start = ((), (), s32[]{:S(2)}) async-start(), calls=%async_computation.38 | async-start | bytes 557056
  1645.8 817.5 %all-reduce.18.cloned.1.call-start = ((), (), s32[]{:S(2)}) async-start(), calls=%async_computation.47 | async-start | bytes 4194304 | tf_op jit(solution)/shard_map/psum | solution.py:454
  (149 other events, 5566.2 us)
Sparse Core Ops, SparseCore 0:
  156.8 55.2 all-gather.18
  214.9 55.4 all-gather.36
  459.8 65.5 all-gather.28
  527.9 103.3 all-reduce.23
  633.4 66.9 all-gather.24
  702.7 65.3 all-gather.26
  914.1 103.5 all-reduce.21
  1058.3 80.5 reduce-scatter.36
  1143.4 78.8 reduce-scatter.40
  1226.0 63.8 reduce-scatter.42
  1294.0 64.4 reduce-scatter.38
  1361.5 73.9 all-reduce.19
  1438.7 72.1 all-reduce.15
  1596.6 67.5 reduce-scatter.52
  1667.9 67.7 reduce-scatter.54
  1739.4 67.7 reduce-scatter.56
  1811.0 65.6 reduce-scatter.50
  1881.1 67.7 reduce-scatter.44
  1953.5 86.0 reduce-scatter.60
  2044.2 85.6 reduce-scatter.58
  2134.6 85.6 reduce-scatter.62
  2224.3 63.8 reduce-scatter.46
  2292.0 64.3 reduce-scatter.48
  2359.2 104.1 all-reduce.17
  (11 shorter events, 485.0 us)
where the time goes:
time: 2560 us; the launch traced here: 2550 us
  waiting for transfers between devices  1460 us (57%)
  matrix products  431 us (17%)
  local copies, waits for them, and re-layouts  227 us (9%)
  blocking collectives  225 us (9%)
  other arithmetic  181 us (7%)
    unnamed x43, waiting for transfers between devices  552 us
    unnamed x306, local copies, waits for them, and re-layouts  149 us
    psum x1, waiting for transfers between devices, local(): lax.psum(d_normed_in.astype(jnp.bfloat16), 'col').astype(jnp.float32)  105 us
    psum x1, waiting for transfers between devices, local(): d_mid_full = lax.psum(d_mid.astype(jnp.bfloat16), 'col').astype(jnp.float32)  104 us
    reduce_scatter x2, waiting for transfers between devices, local(): lax.psum_scatter(d_key_pack.astype(jnp.bfloat16), 'row', scatter_dimensio...  97 us
    reduce_scatter x2, waiting for transfers between devices, local(): lax.psum_scatter(d_rope_keys.astype(jnp.bfloat16), 'row', scatter_dimensi...  93 us
    psum x1, waiting for transfers between devices, local(): lax.psum(attn_part.astype(jnp.bfloat16), 'col').astype(jnp.float32)  89.3 us
    reduce_scatter x1, waiting for transfers between devices, reduce_grads(): lax.psum_scatter(grads[0].astype(jnp.bfloat16), 'row', scatter_dimension=...  70.6 us
  transfers between devices with their start and end apart: 35, of which 26 were waited for; matrix products, arithmetic and copies ran while one was open for 30% of the time, Pallas kernels for 0%

commit v1 on v0

v1 whole, which is shorter than its diff:
```python
import jax
import jax.numpy as jnp
from jax import lax
from jax.experimental import pallas as pl
from jax.experimental.pallas import tpu as pltpu
from jax.sharding import PartitionSpec as P

D = 2048
NOPE = 128
ROPE = 64
QK = NOPE + ROPE
VDIM = 128
KVL = 512
TOPK = 6
EXPERTS = 8
MICRO = 2
TRUNK = 1024
BLK = 256
SEGS = 13
ROWS = 16
COLS = 8
TOK = MICRO * BLK
OWN = TOK // COLS
FEAT = D // COLS
QUART = 4
SHARED = 352
ROUTED = 176
HID = 1792
LAT = KVL + ROPE
LATC = LAT // COLS
SCALE = QK**-0.5
EPS = 1e-06
THETA = 10000.0
NEG = -1e30
MIB = 1024 * 1024
F32 = jnp.float32
BF16 = jnp.bfloat16
NT = (((1,), (1,)), ((), ()))
TN = (((0,), (0,)), ((), ()))


def inverse_rms(values):
    return lax.rsqrt(jnp.mean(values * values, axis=-1, keepdims=True) + EPS)


def norm_backward(grad_out, values, inv_scale, norm_gain):
    weighted = grad_out * norm_gain
    inner = jnp.mean(weighted * values, axis=-1, keepdims=True)
    return inv_scale * weighted - values * (inv_scale * inv_scale * inv_scale) * inner


def rotate(values, cos_table, sin_table):
    half = values.shape[-1] // 2
    a, b = values[..., :half], values[..., half:]
    return jnp.concatenate(
        [a * cos_table - b * sin_table, a * sin_table + b * cos_table], axis=-1
    )


def matmul(a, b):
    return jnp.dot(a, b, preferred_element_type=F32)


def matmul_nt(a, b):
    return lax.dot_general(a, b, NT, preferred_element_type=F32)


def matmul_tn(a, b):
    return lax.dot_general(a, b, TN, preferred_element_type=F32)


def swap(values, axis, groups=None):
    return lax.all_to_all(values, axis, 0, 0, tiled=True, axis_index_groups=groups)


def share(values, axis, count):
    return swap(jnp.broadcast_to(values[None], (count,) + values.shape), axis)


def depth_kernel(parents_ref, seg_ref, out_ref):
    seg = seg_ref[0]
    for m in range(MICRO):

        def climb(step, state):
            at, count = state
            return parents_ref[m, at], count + (at > 0).astype(jnp.int32)

        _, count = lax.fori_loop(0, SEGS, climb, (parents_ref[m, seg], jnp.int32(0)))
        out_ref[m] = count


def ancestor_depths(parents, seg):
    smem = pl.BlockSpec(memory_space=pltpu.SMEM)
    return pl.pallas_call(
        depth_kernel,
        out_shape=jax.ShapeDtypeStruct((MICRO,), jnp.int32),
        in_specs=[smem, smem],
        out_specs=smem,
    )(parents, seg)


def list_ancestors(meta, qb, listed):
    def climb(step, state):
        at, count = state
        listed[count] = at + 3
        return meta[at], count + (at > 0).astype(jnp.int32)

    _, count = lax.fori_loop(0, SEGS, climb, (meta[qb - 3], jnp.int32(0)))
    return count


def causal_mask():
    key = lax.broadcasted_iota(jnp.int32, (BLK, BLK), 0)
    query = lax.broadcasted_iota(jnp.int32, (BLK, BLK), 1)
    return key <= query


def attend_kernel(meta, q_ref, k_ref, vt_ref, o_ref, lse_ref, listed):
    quarter = meta[SEGS]
    for i in range(QUART):
        qb = QUART * i + quarter
        q = q_ref[i]
        s = matmul_nt(k_ref[qb], q) * SCALE
        s = jnp.where(causal_mask(), s, NEG)
        top = jnp.max(s, axis=0, keepdims=True)
        p = jnp.exp(s - top)
        total = jnp.sum(p, axis=0, keepdims=True)
        out = matmul(vt_ref[qb], p.astype(BF16))

        def step(kb, state):
            top, total, out = state
            s = matmul_nt(k_ref[kb], q) * SCALE
            new_top = jnp.maximum(top, jnp.max(s, axis=0, keepdims=True))
            shrink = jnp.exp(top - new_top)
            p = jnp.exp(s - new_top)
            total = total * shrink + jnp.sum(p, axis=0, keepdims=True)
            out = out * shrink + matmul(vt_ref[kb], p.astype(BF16))
            return new_top, total, out

        state = (top, total, out)
        if i == 0:
            state = lax.fori_loop(0, quarter, step, state)
        else:
            for kb in range(TRUNK // BLK):
                state = step(kb, state)
            count = list_ancestors(meta, qb, listed)
            state = lax.fori_loop(0, count, lambda t, c: step(listed[t], c), state)
        top, total, out = state
        o_ref[i] = (out * (1.0 / total)).T.astype(BF16)
        lse_ref[i] = top + jnp.log(total)


def attend(meta, q, k, vt):
    smem = pl.BlockSpec(memory_space=pltpu.SMEM)
    vmem = pl.BlockSpec(memory_space=pltpu.VMEM)
    pairs = 32 * BLK * BLK
    return pl.pallas_call(
        attend_kernel,
        out_shape=(
            jax.ShapeDtypeStruct((QUART, BLK, VDIM), BF16),
            jax.ShapeDtypeStruct((QUART, 1, BLK), F32),
        ),
        in_specs=[smem, vmem, vmem, vmem],
        out_specs=(vmem, vmem),
        scratch_shapes=[pltpu.SMEM((16,), jnp.int32)],
        compiler_params=pltpu.CompilerParams(vmem_limit_bytes=32 * MIB),
        cost_estimate=pl.CostEstimate(
            flops=pairs * 2 * (QK + VDIM), bytes_accessed=4 * MIB, transcendentals=pairs
        ),
    )(meta, q, k, vt)


def attend_back_kernel(
    meta, q_ref, k_ref, kt_ref, v_ref, o_ref, lse_ref, do_ref, dq_ref, dkv_ref, dk, dv, listed
):
    quarter = meta[SEGS]
    dk[...] = jnp.zeros_like(dk)
    dv[...] = jnp.zeros_like(dv)
    for i in range(QUART):
        qb = QUART * i + quarter
        q = q_ref[i]
        do = do_ref[i]
        lse = lse_ref[i]
        pairs = do.astype(F32) * o_ref[i].astype(F32)
        delta = jnp.sum(pairs.T, axis=0, keepdims=True)

        def step(kb, dqt, masked=False):
            s = matmul_nt(k_ref[kb], q) * SCALE
            p = jnp.exp(s - lse)
            if masked:
                p = jnp.where(causal_mask(), p, 0.0)
            dp = matmul_nt(v_ref[kb], do)
            ds = (p * (dp - delta) * SCALE).astype(BF16)
            dv[kb] += matmul(p.astype(BF16), do)
            dk[kb] += matmul(ds, q)
            return dqt + matmul(kt_ref[kb], ds)

        dqt = step(qb, jnp.zeros((QK, BLK), F32), True)
        if i == 0:
            dqt = lax.fori_loop(0, quarter, step, dqt)
        else:
            for kb in range(TRUNK // BLK):
                dqt = step(kb, dqt)
            count = list_ancestors(meta, qb, listed)
            dqt = lax.fori_loop(0, count, lambda t, c: step(listed[t], c), dqt)
        dq_ref[i] = dqt.T.astype(BF16)
    dkv_ref[:, :, :NOPE] = dk[:, :, :NOPE].astype(BF16)
    dkv_ref[:, :, NOPE : NOPE + VDIM] = dv[...].astype(BF16)
    dkv_ref[:, :, NOPE + VDIM :] = dk[:, :, NOPE:].astype(BF16)


def attend_back(meta, q, k, kt, v, o, lse, do):
    smem = pl.BlockSpec(memory_space=pltpu.SMEM)
    vmem = pl.BlockSpec(memory_space=pltpu.VMEM)
    pairs = 32 * BLK * BLK
    return pl.pallas_call(
        attend_back_kernel,
        out_shape=(
            jax.ShapeDtypeStruct((QUART, BLK, QK), BF16),
            jax.ShapeDtypeStruct((ROWS, BLK, QK + VDIM), BF16),
        ),
        in_specs=[smem] + [vmem] * 7,
        out_specs=(vmem, vmem),
        scratch_shapes=[
            pltpu.VMEM((ROWS, BLK, QK), F32),
            pltpu.VMEM((ROWS, BLK, VDIM), F32),
            pltpu.SMEM((16,), jnp.int32),
        ],
        compiler_params=pltpu.CompilerParams(vmem_limit_bytes=40 * MIB),
        cost_estimate=pl.CostEstimate(
            flops=pairs * 2 * (3 * QK + 2 * VDIM), bytes_accessed=10 * MIB, transcendentals=pairs
        ),
    )(meta, q, k, kt, v, o, lse, do)


def hidden_kernel(mid_ref, grad_ref, gate_ref, spread_ref, wg_ref, wu_ref, wd_ref, out_ref):
    mid = mid_ref[...]
    pre = matmul(mid, wg_ref[...])
    up = matmul(mid, wu_ref[...])
    back = matmul(grad_ref[...], wd_ref[...])
    gate = matmul(gate_ref[...], spread_ref[...])
    sig = 1.0 / (1.0 + jnp.exp(-pre))
    act = pre * sig
    back = back * gate
    out_ref[0] = (back * up * (sig * (1.0 + pre * (1.0 - sig)))).astype(BF16)
    out_ref[1] = (back * act).astype(BF16)
    out_ref[2] = (act * up * gate).astype(BF16)


def hidden(mid, grad, gates, spread, weights):
    whole = pl.BlockSpec((TOK, D), lambda j: (0, 0))
    parts = HID // BLK

    def weight(at):
        return pl.BlockSpec((D, BLK), lambda j: (0, at * parts + j))

    return pl.pallas_call(
        hidden_kernel,
        grid=(parts,),
        out_shape=jax.ShapeDtypeStruct((3, TOK, HID), BF16),
        in_specs=[
            whole,
            whole,
            pl.BlockSpec(gates.shape, lambda j: (0, 0)),
            pl.BlockSpec((spread.shape[0], BLK), lambda j: (0, j)),
            weight(0),
            weight(1),
            weight(2),
        ],
        out_specs=pl.BlockSpec((3, TOK, BLK), lambda j: (0, 0, j)),
        compiler_params=pltpu.CompilerParams(vmem_limit_bytes=48 * MIB),
        cost_estimate=pl.CostEstimate(
            flops=2 * TOK * D * HID * 3, bytes_accessed=32 * MIB, transcendentals=TOK * HID
        ),
    )(mid, grad, gates, spread, weights, weights, weights)


def model_kernel(hid_ref, w_ref, out_ref, back_ref):
    back = matmul_nt(hid_ref[0], w_ref[:, :HID]) + matmul_nt(hid_ref[1], w_ref[:, HID : 2 * HID])
    back_ref[...] = back.astype(BF16)
    out_ref[0] = matmul_nt(hid_ref[2], w_ref[:, 2 * HID :]).astype(BF16)


def model(hid, weights):
    return pl.pallas_call(
        model_kernel,
        grid=(COLS,),
        out_shape=(
            jax.ShapeDtypeStruct((COLS, TOK, FEAT), BF16),
            jax.ShapeDtypeStruct((TOK, D), BF16),
        ),
        in_specs=[
            pl.BlockSpec((3, TOK, HID), lambda j: (0, 0, 0)),
            pl.BlockSpec((FEAT, 3 * HID), lambda j: (j, 0)),
        ],
        out_specs=(
            pl.BlockSpec((1, TOK, FEAT), lambda j: (j, 0, 0)),
            pl.BlockSpec((TOK, FEAT), lambda j: (0, j)),
        ),
        compiler_params=pltpu.CompilerParams(vmem_limit_bytes=48 * MIB),
        cost_estimate=pl.CostEstimate(
            flops=2 * TOK * D * HID * 3, bytes_accessed=32 * MIB, transcendentals=0
        ),
    )(hid, weights)


def weight_grad_kernel(mid_ref, grad_ref, hid_ref, out_ref):
    part = pl.program_id(0)

    @pl.when(part < 2)
    def _():
        out_ref[...] = matmul(mid_ref[...], hid_ref[0]).astype(BF16)

    @pl.when(part == 2)
    def _():
        out_ref[...] = matmul(grad_ref[...], hid_ref[0]).astype(BF16)


def weight_grads(mid_t, grad_t, hid):
    parts = HID // BLK
    whole = pl.BlockSpec((D, TOK), lambda s, j: (0, 0))
    return pl.pallas_call(
        weight_grad_kernel,
        grid=(3, parts),
        out_shape=jax.ShapeDtypeStruct((D, 3 * HID), BF16),
        in_specs=[whole, whole, pl.BlockSpec((1, TOK, BLK), lambda s, j: (s, 0, j))],
        out_specs=pl.BlockSpec((D, BLK), lambda s, j: (0, s * parts + j)),
        compiler_params=pltpu.CompilerParams(vmem_limit_bytes=48 * MIB),
        cost_estimate=pl.CostEstimate(
            flops=2 * TOK * D * HID * 3, bytes_accessed=32 * MIB, transcendentals=0
        ),
    )(mid_t, grad_t, hid)


def pack_hidden(shared, routed):
    rows = shared.shape[0]
    return jnp.concatenate(
        [
            shared,
            jnp.swapaxes(routed, 0, 1).reshape(rows, EXPERTS * ROUTED),
            jnp.zeros((rows, HID - SHARED - EXPERTS * ROUTED), routed.dtype),
        ],
        axis=1,
    )


def local(
    tokens,
    out_grad,
    parents,
    routes,
    gates,
    norm_in,
    w_query,
    w_latent,
    norm_latent,
    w_expand,
    w_output,
    norm_mid,
    w_shared_gate,
    w_shared_up,
    w_shared_down,
    w_expert_gate,
    w_expert_up,
    w_expert_down,
):
    row = lax.axis_index("row")
    col = lax.axis_index("col")
    quarter = row % QUART
    quarter_groups = [[QUART * i + k for i in range(QUART)] for k in range(QUART)]
    own_start = col * OWN
    gain_in = norm_in.astype(F32)
    gain_latent = norm_latent.astype(F32)
    gain_mid = norm_mid.astype(F32)
    heads = 2

    query_pack = w_query.reshape(D // ROWS, heads, QK)
    attn_pack = jnp.concatenate(
        [
            query_pack[:, :, :NOPE].reshape(D // ROWS, heads * NOPE),
            query_pack[:, :, NOPE:].reshape(D // ROWS, heads * ROPE),
            w_output.T,
            w_expand.reshape(D // ROWS, D // ROWS),
            w_latent,
            jnp.zeros((D // ROWS, 128 - LATC), BF16),
        ],
        axis=1,
    )
    ffn_pack = jnp.concatenate(
        [
            pack_hidden(w_shared_gate, w_expert_gate),
            pack_hidden(w_shared_up, w_expert_up),
            pack_hidden(w_shared_down.T, jnp.swapaxes(w_expert_down, 1, 2)),
        ],
        axis=1,
    )
    attn_full = lax.all_gather(attn_pack, "row", axis=0, tiled=True)
    ffn_full = lax.all_gather(ffn_pack, "row", axis=0, tiled=True)
    query_full = attn_full[:, : heads * QK]
    output_full = attn_full[:, 384:640]
    expand_full = attn_full[:, 640:768].reshape(KVL, heads * (NOPE + VDIM))
    latent_full = attn_full[:, 768 : 768 + LATC]

    seg = jnp.maximum(row - (TRUNK // BLK - 1), 0).astype(jnp.int32)
    depths = ancestor_depths(parents, seg.reshape(1))
    starts = jnp.where(seg > 0, TRUNK + BLK * depths, BLK * row)
    positions = (starts[:, None] + jnp.arange(BLK, dtype=jnp.int32)[None, :]).reshape(TOK)
    frequency = THETA ** (-jnp.arange(ROPE // 2, dtype=F32) / (ROPE // 2))
    angles = positions.astype(F32)[:, None] * frequency[None, :]
    cos_table, sin_table = jnp.cos(angles), jnp.sin(angles)

    inputs = share(tokens.reshape(TOK, FEAT), "col", COLS).transpose(1, 0, 2).reshape(TOK, D)
    inputs_float = inputs.astype(F32)
    scale_in = inverse_rms(inputs_float)
    normed_in = (inputs_float * scale_in * gain_in).astype(BF16)
    latent_part = matmul(normed_in, latent_full).astype(BF16)
    latent = share(latent_part, "col", COLS).transpose(1, 0, 2).reshape(TOK, LAT)
    query_pre = matmul(normed_in, query_full)
    query_nope = query_pre[:, : heads * NOPE].reshape(TOK, heads, NOPE)
    query_rope = rotate(
        query_pre[:, heads * NOPE :].reshape(TOK, heads, ROPE),
        cos_table[:, None, :],
        sin_table[:, None, :],
    )
    query = jnp.concatenate([query_nope, query_rope], axis=-1).astype(BF16)
    query = query.reshape(MICRO, BLK, heads, QK).transpose(2, 0, 1, 3)
    query = swap(query.reshape(heads * MICRO, BLK, QK), "row", quarter_groups)
    compressed = latent[:, :KVL].astype(F32)
    scale_latent = inverse_rms(compressed)
    latent_normed = (compressed * scale_latent * gain_latent).astype(BF16)
    expanded = matmul(latent_normed, expand_full).astype(BF16)
    rope_keys = rotate(latent[:, KVL:].astype(F32), cos_table, sin_table).astype(BF16)
    pack = jnp.concatenate(
        [
            expanded.reshape(MICRO, BLK, heads, NOPE + VDIM).transpose(2, 0, 1, 3),
            jnp.broadcast_to(rope_keys.reshape(1, MICRO, BLK, ROPE), (heads, MICRO, BLK, ROPE)),
        ],
        axis=-1,
    ).reshape(heads * MICRO, 1, BLK, QK + VDIM)
    pack = jnp.broadcast_to(pack, (heads * MICRO, QUART, BLK, QK + VDIM))
    pack = swap(pack.reshape(ROWS, BLK, QK + VDIM), "row")

    keys = jnp.concatenate([pack[:, :, :NOPE], pack[:, :, NOPE + VDIM :]], axis=-1)
    values = pack[:, :, NOPE : NOPE + VDIM]
    keys_t = jnp.swapaxes(keys, 1, 2)
    values_t = jnp.swapaxes(values, 1, 2)
    tree = (row // QUART) % MICRO
    own_parents = lax.dynamic_index_in_dim(parents, tree, 0, keepdims=False)
    meta = jnp.concatenate([own_parents, quarter.astype(jnp.int32).reshape(1)])
    attended_own, lse = attend(meta, query, keys, values_t)

    def to_heads(blocks):
        width = blocks.shape[-1]
        blocks = swap(blocks, "row", quarter_groups).reshape(heads, MICRO, BLK, width)
        return blocks.transpose(1, 2, 0, 3).reshape(TOK, heads, width)

    attended = to_heads(attended_own).reshape(TOK, heads * VDIM)

    attn_part = matmul_nt(attended, output_full).astype(BF16)
    attn_sum = jnp.sum(swap(attn_part.reshape(COLS, OWN, D), "col").astype(F32), axis=0)
    own_inputs = lax.dynamic_slice_in_dim(inputs, own_start, OWN, 0).astype(F32)
    residual = own_inputs + attn_sum
    scale_mid = inverse_rms(residual)
    normed_own = (residual * scale_mid * gain_mid).astype(BF16)
    normed_mid = share(normed_own, "col", COLS).reshape(TOK, D)

    grad_full = share(out_grad.reshape(TOK, FEAT), "col", COLS).transpose(1, 0, 2).reshape(TOK, D)
    named = routes.reshape(TOK, TOPK, 1) == jnp.arange(EXPERTS, dtype=jnp.int32)
    gate_of = jnp.sum(jnp.where(named, gates.reshape(TOK, TOPK, 1), 0.0), axis=1)
    gate_of = jnp.concatenate(
        [jnp.ones((TOK, 1), F32), gate_of, jnp.zeros((TOK, 15 - EXPERTS), F32)], axis=1
    )
    gate_high = gate_of.astype(BF16)
    gate_low = (gate_of - gate_high.astype(F32)).astype(BF16)
    unit = jnp.arange(HID, dtype=jnp.int32)
    group = jnp.where(unit < SHARED, 0, 1 + (unit - SHARED) // ROUTED)
    spread = (group[None, :] == jnp.arange(16, dtype=jnp.int32)[:, None]).astype(BF16)
    hid = hidden(
        normed_mid,
        grad_full,
        jnp.concatenate([gate_high, gate_low], axis=1),
        jnp.concatenate([spread, spread], axis=0),
        ffn_full,
    )
    out_part, mid_part = model(hid, ffn_full)
    d_mid = jnp.sum(swap(mid_part.reshape(COLS, OWN, D), "col").astype(F32), axis=0)
    mid_gain = jnp.sum(d_mid * residual * scale_mid, axis=0)
    own_grad = lax.dynamic_slice_in_dim(grad_full, own_start, OWN, 0).astype(F32)
    d_residual = own_grad + norm_backward(d_mid, residual, scale_mid, gain_mid)
    d_low = share(d_residual.astype(BF16), "col", COLS).reshape(TOK, D)

    def by_feature(own):
        return own.reshape(OWN, COLS, FEAT).transpose(1, 0, 2)

    own_part = lax.dynamic_slice_in_dim(out_part, own_start, OWN, 1)
    own_part = (own_part.astype(F32) + by_feature(residual)).astype(BF16)
    out_part = lax.dynamic_update_slice_in_dim(out_part, own_part, own_start, 1)
    layer_out = jnp.sum(swap(out_part, "col").astype(F32), axis=0).astype(BF16)

    ffn_grads = weight_grads(normed_mid.T, grad_full.T, hid)
    ffn_grads = lax.psum_scatter(ffn_grads, "row", scatter_dimension=0, tiled=True)

    d_attended = matmul(d_low, output_full).astype(BF16)
    d_attended = d_attended.reshape(MICRO, BLK, heads, VDIM).transpose(2, 0, 1, 3)
    d_attended = swap(d_attended.reshape(heads * MICRO, BLK, VDIM), "row", quarter_groups)
    d_query, d_pack = attend_back(
        meta, query, keys, keys_t, values, attended_own, lse, d_attended
    )
    d_query = to_heads(d_query)
    d_query_rope = rotate(
        d_query[:, :, NOPE:].astype(F32), cos_table[:, None, :], -sin_table[:, None, :]
    ).astype(BF16)
    d_query_pre = jnp.concatenate(
        [
            d_query[:, :, :NOPE].reshape(TOK, heads * NOPE),
            d_query_rope.reshape(TOK, heads * ROPE),
        ],
        axis=1,
    )
    d_pack = swap(d_pack, "row").reshape(heads, MICRO, QUART, BLK, QK + VDIM)
    d_pack = jnp.sum(d_pack.astype(F32), axis=2)
    d_expanded = d_pack[..., : NOPE + VDIM].transpose(1, 2, 0, 3)
    d_expanded = d_expanded.reshape(TOK, heads * (NOPE + VDIM)).astype(BF16)
    d_rope_keys = jnp.sum(d_pack[..., NOPE + VDIM :], axis=0).reshape(TOK, ROPE)

    d_latent_normed = matmul_nt(d_expanded, expand_full)
    latent_gain = jnp.sum(d_latent_normed * compressed * scale_latent, axis=0)
    d_latent = jnp.concatenate(
        [
            norm_backward(d_latent_normed, compressed, scale_latent, gain_latent),
            rotate(d_rope_keys, cos_table, -sin_table),
        ],
        axis=1,
    ).astype(BF16)
    d_latent = swap(d_latent.reshape(TOK, COLS, LATC).transpose(1, 0, 2), "col")
    d_latent = jnp.sum(d_latent.astype(F32), axis=0).astype(BF16)

    d_in = matmul_nt(d_query_pre, query_full) + matmul_nt(d_latent, latent_full)
    in_gain = jnp.sum(d_in * inputs_float * scale_in, axis=0)
    d_tokens = norm_backward(d_in, inputs_float, scale_in, gain_in)
    own_tokens = lax.dynamic_slice_in_dim(d_tokens, own_start, OWN, 0) + d_residual
    d_tokens = lax.dynamic_update_slice_in_dim(d_tokens, own_tokens, own_start, 0)
    d_tokens = d_tokens.astype(BF16).reshape(TOK, COLS, FEAT).transpose(1, 0, 2)
    input_grad = jnp.sum(swap(d_tokens, "col").astype(F32), axis=0).astype(BF16)

    attn_grads = jnp.concatenate(
        [
            matmul_tn(normed_in, d_query_pre).astype(BF16),
            matmul_tn(d_low, attended).astype(BF16),
            matmul_tn(latent_normed, d_expanded).astype(BF16).reshape(D, D // ROWS),
            matmul_tn(normed_in, d_latent).astype(BF16),
            jnp.zeros((D, 128 - LATC), BF16),
        ],
        axis=1,
    )
    attn_grads = swap(attn_grads.reshape(ROWS, D // ROWS, attn_grads.shape[1]), "row")
    attn_grads = jnp.sum(attn_grads.astype(F32), axis=0)
    grad_query = jnp.concatenate(
        [
            attn_grads[:, : heads * NOPE].reshape(-1, heads, NOPE),
            attn_grads[:, heads * NOPE : heads * QK].reshape(-1, heads, ROPE),
        ],
        axis=-1,
    ).reshape(-1, heads * QK)
    grad_output = attn_grads[:, 384:640].T
    grad_expand = attn_grads[:, 640:768].reshape(KVL // ROWS, heads * (NOPE + VDIM))
    grad_latent = attn_grads[:, 768 : 768 + LATC]

    def unpack(at):
        part = ffn_grads[:, at * HID : (at + 1) * HID].astype(F32)
        routed = part[:, SHARED : SHARED + EXPERTS * ROUTED]
        return part[:, :SHARED], routed.reshape(-1, EXPERTS, ROUTED)

    grad_shared_gate, grad_expert_gate = unpack(0)
    grad_shared_up, grad_expert_up = unpack(1)
    grad_shared_down, grad_expert_down = unpack(2)

    world = ("row", "col")
    gain = jnp.concatenate([in_gain, latent_gain, mid_gain]).reshape(ROWS * COLS, -1)
    gain = jnp.sum(swap(gain, world), axis=0)
    gain = share(gain, world, ROWS * COLS).reshape(-1)
    return (
        layer_out.reshape(MICRO, BLK, FEAT),
        input_grad.reshape(MICRO, BLK, FEAT),
        gain[:D],
        grad_query,
        grad_latent,
        gain[D : D + KVL],
        grad_expand,
        grad_output,
        gain[D + KVL :],
        grad_shared_gate,
        grad_shared_up,
        grad_shared_down.T,
        jnp.swapaxes(grad_expert_gate, 0, 1),
        jnp.swapaxes(grad_expert_up, 0, 1),
        grad_expert_down.transpose(1, 2, 0),
    )


def solution(mesh):
    in_specs = (
        P(None, "row", "col"),
        P(None, "row", "col"),
        P(),
        P(None, "row", None),
        P(None, "row", None),
        P(),
        P("row", "col"),
        P("row", "col"),
        P(),
        P("row", "col"),
        P("col", "row"),
        P(),
        P("row", "col"),
        P("row", "col"),
        P("col", "row"),
        P(None, "row", "col"),
        P(None, "row", "col"),
        P(None, "col", "row"),
    )
    out_specs = (
        P(None, "row", "col"),
        P(None, "row", "col"),
        P(),
        P("row", "col"),
        P("row", "col"),
        P(),
        P("row", "col"),
        P("col", "row"),
        P(),
        P("row", "col"),
        P("row", "col"),
        P("col", "row"),
        P(None, "row", "col"),
        P(None, "row", "col"),
        P(None, "col", "row"),
    )
    return jax.shard_map(local, mesh=mesh, in_specs=in_specs, out_specs=out_specs, check_vma=False)
```

time: 2560 us -> 783 us (0.31)
  waiting for transfers between devices: 1460 us -> 337 us
  matrix products: 431 us -> 27.3 us
  blocking collectives: 225 us -> 71.5 us
  other arithmetic: 181 us -> 50.2 us
  local copies, waits for them, and re-layouts: 227 us -> 106 us
  starting transfers between devices: 3.38 us -> 84.4 us
  Pallas kernels: 0 us -> 78.5 us
    unnamed x43 -> x3, waiting for transfers between devices: 552 us -> 0.05 us
    dot_general x111 -> x12, matrix products: 431 us -> 27.3 us  [the longest x4 15.2 us: matmul_nt(): return lax.dot_general(a, b, NT, preferred_element_type=F32)]
    reduce_scatter x8 -> x1, waiting for transfers between devices: 326 us -> 0.01 us  [local(): lax.psum_scatter(ffn_grads, 'row', scatter_dimension=0, tiled=True)]
    all_to_all x0 -> x16, waiting for transfers between devices: none -> 309 us  [swap(): lax.all_to_all(values, axis, 0, 0, tiled=True, axis_index_groups=groups)]
    psum x5 -> x0, waiting for transfers between devices: 299 us -> none  [the longest x1 105 us: local(): lax.psum(d_normed_in.astype(jnp.bfloat16), 'col').astype(jnp.float32)]
    all_gather x14 -> x2, waiting for transfers between devices: 285 us -> 27.3 us  [the longest x1 27.3 us: local(): attn_full = lax.all_gather(attn_pack, 'row', axis=0, tiled=True)]
    all_gather x6 -> x0, blocking collectives: 157 us -> none  [the longest x2 57.5 us: local(): latent = lax.all_gather(latent_part, 'col', axis=1, tiled=True)]
    unnamed x306 -> x169, local copies, waits for them, and re-layouts: 149 us -> 29.9 us
  transfers between devices with their start and end apart: 35 -> 19, of which waited for: 26 -> 16; matrix products, arithmetic and copies ran while one was open for 30% -> 20% of each run, Pallas kernels for 0% -> 5%
where the time goes in v1:
time: 783 us; the launch traced here: 770 us
  waiting for transfers between devices  337 us (43%)
  local copies, waits for them, and re-layouts  106 us (14%)
  starting transfers between devices  84.4 us (11%)
  Pallas kernels  78.5 us (10%)
  blocking collectives  71.5 us (9%)
  other arithmetic  50.2 us (6%)
  matrix products  27.3 us (3%)
  between operations  15.5 us (2%)
    all_to_all x16, waiting for transfers between devices, swap(): lax.all_to_all(values, axis, 0, 0, tiled=True, axis_index_groups=groups)  309 us
    all_to_all x16, starting transfers between devices, swap(): lax.all_to_all(values, axis, 0, 0, tiled=True, axis_index_groups=groups)  84.3 us
    all_to_all x3, blocking collectives, swap(): lax.all_to_all(values, axis, 0, 0, tiled=True, axis_index_groups=groups)  71.5 us
    unnamed x169, local copies, waits for them, and re-layouts  29.9 us
    all_gather x1, waiting for transfers between devices, local(): attn_full = lax.all_gather(attn_pack, 'row', axis=0, tiled=True)  27.3 us
    pallas_call x1, Pallas kernels, weight_grads(): pl.pallas_call(weight_grad_kernel, grid=(3, parts), out_shape=jax.ShapeDt...  22.3 us
    pallas_call x1, Pallas kernels, model(): pl.pallas_call(model_kernel, grid=(COLS,), out_shape=(jax.ShapeDtypeStruc...  18.4 us
    pallas_call x1, Pallas kernels, hidden(): pl.pallas_call(hidden_kernel, grid=(parts,), out_shape=jax.ShapeDtypeStru...  17.3 us
  transfers between devices with their start and end apart: 19, of which 16 were waited for; matrix products, arithmetic and copies ran while one was open for 20% of the time, Pallas kernels for 5%

profile of v1, /device:TPU:0, one launch (start us, length us, event | category | flops | bytes accessed | tf_op | source)
XLA Modules:
  0.0 770.2 jit_solution(5317706120840924690)
XLA Ops:
  26.8 29.1 %all-to-all-done = bf16[8,512,256]{1,2,0:T(8,128)(2,1)S(1)} async-done(((bf16[8,512,256]{1,2,0:T(8,128)(2,1)}), bf16[8,512,256]{1,2,0:T(8,128)(2,1)S(1)}, u32[]{:S(2)}, u32[]{:S(2)}) %all-to-all-start) | async-done | bytes 2097184 | tf_op jit(solution)/shard_map/all_to_all | solution.py:73
  59.0 27.3 %all-gather.3.cloned.1.call-done = bf16[2048,896]{0,1:T(8,128)(2,1)} async-done(((bf16[128,896]{0,1:T(8,128)(2,1)}), bf16[2048,896]{0,1:T(8,128)(2,1)}) %all-gather.3.cloned.1.call-update) | async-done | bytes 3670032 | tf_op jit(solution)/shard_map/all_gather | solution.py:397
  112.3 8.7 %all-to-all-done.1 = bf16[4,256,192]{1,2,0:T(8,128)(2,1)S(1)} async-done(((bf16[4,256,192]{1,2,0:T(8,128)(2,1)}), bf16[4,256,192]{1,2,0:T(8,128)(2,1)S(1)}, u32[]{:S(2)}, u32[]{:S(2)}) %all-to-all-start.1) | async-done | bytes 393248 | tf_op jit(solution)/shard_map/all_to_all | solution.py:73
  129.4 47.6 %all-to-all-done.3 = bf16[16,256,320]{1,2,0:T(8,128)(2,1)S(1)} async-done(((bf16[16,256,320]{1,2,0:T(8,128)(2,1)}), bf16[16,256,320]{1,2,0:T(8,128)(2,1)S(1)}, u32[]{:S(2)}, u32[]{:S(2)}) %all-to-all-start.3) | async-done | bytes 2621472 | tf_op jit(solution)/shard_map/all_to_all | solution.py:73
  187.8 8.8 %shard_map.290 = (bf16[4,256,128]{2,1,0:T(8,128)(2,1)S(1)}, f32[4,1,256]{2,1,0:T(1,128)S(1)}) custom-call(s32[14]{0:T(128)S(1)} %pad_add_fusion.meta, bf16[4,256,192]{2,1,0:T(8,128)(2,1)S(1)} %copy-done.10, bf16[16,256,192]{2,1,0:T(8,128)(2,1)S(1)} %copy.283.k_ref, bf16[16,128,256]{2,1,0:T(8,128)(2,1)S(1)} %get-tuple-element.126.vt_ref), custom_call_target="tpu_custom_call" | custom-call | flops 1342177280 | bytes 4194304 | tf_op jit(solution)/shard_map/pallas_call | solution.py:157
  196.7 14.7 %all_to_all.100 = bf16[4,256,128]{2,1,0:T(8,128)(2,1)S(1)} all-to-all(bf16[4,256,128]{2,1,0:T(8,128)(2,1)S(1)} %get-tuple-element.21.o_ref), channel_id=1, replica_groups={{0,32,64,96},{8,40,72,104},{16,48,80,112},{24,56,88,120},{1,33,65,97},{..., dimensions={0} | all-to-all | bytes 524288 | tf_op jit(solution)/shard_map/all_to_all | solution.py:73
  219.4 29.9 %all-to-all-done.5 = bf16[8,64,2048]{2,1,0:T(8,128)(2,1)S(1)} async-done(((bf16[8,64,2048]{2,1,0:T(8,128)(2,1)}), bf16[8,64,2048]{2,1,0:T(8,128)(2,1)S(1)}, u32[]{:S(2)}, u32[]{:S(2)}) %all-to-all-start.5) | async-done | bytes 2097184 | tf_op jit(solution)/shard_map/all_to_all | solution.py:73
  263.2 21.2 %all-to-all-done.7 = bf16[8,512,256]{1,2,0:T(8,128)(2,1)S(1)} async-done(((bf16[8,512,256]{1,2,0:T(8,128)(2,1)}), bf16[8,512,256]{1,2,0:T(8,128)(2,1)S(1)}, u32[]{:S(2)}, u32[]{:S(2)}) %all-to-all-start.7) | async-done | bytes 2097184 | tf_op jit(solution)/shard_map/all_to_all | solution.py:73
  295.3 24.6 %all-to-all-done.6 = bf16[8,64,2048]{2,1,0:T(8,128)(2,1)S(1)} async-done(((bf16[8,64,2048]{2,1,0:T(8,128)(2,1)}), bf16[8,64,2048]{2,1,0:T(8,128)(2,1)S(1)}, u32[]{:S(2)}, u32[]{:S(2)}) %all-to-all-start.6) | async-done | bytes 2097184 | tf_op jit(solution)/shard_map/all_to_all | solution.py:73
  324.0 17.3 %shard_map.291.hid_ref = bf16[3,512,1792]{2,1,0:T(8,128)(2,1)} custom-call(bf16[512,2048]{1,0:T(8,128)(2,1)S(1)} %bitcast.154, bf16[512,2048]{1,0:T(8,128)(2,1)S(1)} %copy-done.3, bf16[512,32]{1,0:T(8,128)(2,1)S(1)} %copy.296.gate_ref, bf16[32,1792]{1,0:T(8,128)(2,1)S(1)} %add_convert_fusion.spread_ref, ...), custom_call_target="tpu_custom_call" | custom-call | flops 11274289152 | bytes 33554432 | tf_op jit(solution)/shard_map/pallas_call | solution.py:257
  341.4 22.3 %shard_map.294 = bf16[2048,5376]{1,0:T(8,128)(2,1)} custom-call(bf16[2048,512]{1,0:T(8,128)(2,1)S(1)} %bitcast.159, bf16[2048,512]{1,0:T(8,128)(2,1)S(1)} %bitcast.156, bf16[3,512,1792]{2,1,0:T(8,128)(2,1)} %shard_map.291.hid_ref), custom_call_target="tpu_custom_call" | custom-call | flops 11274289152 | bytes 33554432 | tf_op jit(solution)/shard_map/pallas_call | solution.py:322
  363.7 18.4 %shard_map.292 = (bf16[8,512,256]{2,1,0:T(8,128)(2,1)S(1)}, bf16[512,2048]{1,0:T(8,128)(2,1)S(1)}) custom-call(bf16[3,512,1792]{2,1,0:T(8,128)(2,1)} %shard_map.291.hid_ref, bf16[2048,5376]{1,0:T(8,128)(2,1)} %all-gather.5.cloned.1.call-done.wg_ref.wu_ref.wd_ref.w_ref), custom_call_target="tpu_custom_call" | custom-call | flops 11274289152 | bytes 33554432 | tf_op jit(solution)/shard_map/pallas_call | solution.py:285
  382.1 27.4 %all_to_all.101 = bf16[8,64,2048]{2,1,0:T(8,128)(2,1)S(1)} all-to-all(bf16[8,64,2048]{2,1,0:T(8,128)(2,1)S(1)} %bitcast.160), channel_id=1, replica_groups=mesh['row'=16,'col'=8] {'col'}, dimensions={0} | all-to-all | bytes 4194304 | tf_op jit(solution)/shard_map/all_to_all | solution.py:73
  418.6 29.4 %all_to_all.102 = bf16[8,64,2048]{2,1,0:T(8,128)(2,1)S(1)} all-to-all(bf16[8,64,2048]{2,1,0:T(8,128)(2,1)S(1)} %broadcast_in_dim.124), channel_id=1, replica_groups=mesh['row'=16,'col'=8] {'col'}, dimensions={0} | all-to-all | bytes 4194304 | tf_op jit(solution)/shard_map/all_to_all | solution.py:73
  459.1 8.6 %all-to-all-done.11.do_ref = bf16[4,256,128]{2,1,0:T(8,128)(2,1)} async-done(((bf16[4,256,128]{2,1,0:T(8,128)(2,1)}), bf16[4,256,128]{2,1,0:T(8,128)(2,1)}, u32[]{:S(2)}, u32[]{:S(2)}) %all-to-all-start.11) | async-done | bytes 262176 | tf_op jit(solution)/shard_map/all_to_all | solution.py:73
  471.7 10.3 %shard_map.293 = (bf16[4,256,192]{2,1,0:T(8,128)(2,1)S(1)}, bf16[16,256,320]{2,1,0:T(8,128)(2,1)S(1)}) custom-call(s32[14]{0:T(128)S(1)} %pad_add_fusion.meta, bf16[4,256,192]{2,1,0:T(8,128)(2,1)S(1)} %copy-done.11, bf16[16,256,192]{2,1,0:T(8,128)(2,1)S(1)} %copy-done.7, bf16[16,192,256]{2,1,0:T(8,128)(2,1)S(1)} %copy-done.9, ...), custom_call_target="tpu_custom_call" | custom-call | flops 3489660928 | bytes 10485760 | tf_op jit(solution)/shard_map/pallas_call | solution.py:216
  511.0 33.6 %all-to-all-done.13 = bf16[16,256,320]{1,2,0:T(8,128)(2,1)} async-done(((bf16[16,256,320]{1,2,0:T(8,128)(2,1)}), bf16[16,256,320]{1,2,0:T(8,128)(2,1)}, u32[]{:S(2)}, u32[]{:S(2)}) %all-to-all-start.13) | async-done | bytes 2621472 | tf_op jit(solution)/shard_map/all_to_all | solution.py:73
  574.8 7.1 fusion.6
  582.6 8.3 %all-to-all-start.16 = ((f32[128,1,36]{2,1,0:T(1,128)}), f32[128,1,36]{2,1,0:T(1,128)S(1)}, u32[]{:S(2)}, u32[]{:S(2)}) async-start(f32[128,1,36]{2,1,0:T(1,128)} %bitcast.209), calls=%async_computation.16 | async-start | bytes 131072 | tf_op jit(solution)/shard_map/all_to_all | solution.py:73
  592.8 7.9 %all-to-all-done.16 = f32[128,1,36]{2,1,0:T(1,128)S(1)} async-done(((f32[128,1,36]{2,1,0:T(1,128)}), f32[128,1,36]{2,1,0:T(1,128)S(1)}, u32[]{:S(2)}, u32[]{:S(2)}) %all-to-all-start.16) | async-done | bytes 18464 | tf_op jit(solution)/shard_map/all_to_all | solution.py:73
  612.2 23.8 %all-to-all-done.8 = bf16[8,512,256]{2,1,0:T(8,128)(2,1)} async-done(((bf16[8,512,256]{2,1,0:T(8,128)(2,1)}), bf16[8,512,256]{2,1,0:T(8,128)(2,1)}, u32[]{:S(2)}, u32[]{:S(2)}) %all-to-all-start.8) | async-done | bytes 2097184 | tf_op jit(solution)/shard_map/all_to_all | solution.py:73
  676.0 17.1 %all-to-all-done.15 = bf16[8,512,256]{1,2,0:T(8,128)(2,1)} async-done(((bf16[8,512,256]{1,2,0:T(8,128)(2,1)}), bf16[8,512,256]{1,2,0:T(8,128)(2,1)}, u32[]{:S(2)}, u32[]{:S(2)}) %all-to-all-start.15) | async-done | bytes 2097184 | tf_op jit(solution)/shard_map/all_to_all | solution.py:73
  693.1 7.1 all-to-all-start.18
  708.3 41.1 %all-to-all-done.18 = bf16[16,128,896]{2,1,0:T(8,128)(2,1)} async-done(((bf16[16,128,896]{2,1,0:T(8,128)(2,1)}), bf16[16,128,896]{2,1,0:T(8,128)(2,1)}, u32[]{:S(2)}, u32[]{:S(2)}) %all-to-all-start.18) | async-done | bytes 3670048 | tf_op jit(solution)/shard_map/all_to_all | solution.py:73
  (352 shorter events, 263.1 us)
Async XLA Ops:
  7.2 79.1 %all-gather.3.cloned.1.call-start = ((), (), s32[]{:S(2)}) async-start(), calls=%async_computation.20 | async-start | bytes 3899392 | tf_op jit(solution)/shard_map/all_gather | solution.py:397
  11.6 310.8 %all-gather.5.cloned.1.call-start = ((), (), s32[]{:S(2)}) async-start(), calls=%async_computation.21 | async-start | bytes 23396352 | tf_op jit(solution)/shard_map/all_gather | solution.py:398
  18.7 37.2 %all-to-all-start = ((bf16[8,512,256]{1,2,0:T(8,128)(2,1)}), bf16[8,512,256]{1,2,0:T(8,128)(2,1)S(1)}, u32[]{:S(2)}, u32[]{:S(2)}) async-start(bf16[8,512,256]{1,2,0:T(8,128)(2,1)} %broadcast_in_dim.53), calls=%async_computation | async-start | bytes 4194304 | tf_op jit(solution)/shard_map/all_to_all | solution.py:73
  24.7 550.0 %copy-start.45 = (f32[2048]{0:T(1024)}, f32[2048]{0:T(1024)S(1)}, u32[]{:S(2)}) copy-start(f32[2048]{0:T(1024)S(1)} %convert_element_type.156) | copy-start | bytes 24580
  59.0 34.9 %copy-start.70 = (bf16[512]{0:T(512)(128)(2,1)S(1)}, bf16[512]{0:T(512)(128)(2,1)}, u32[]{:S(2)}) copy-start(bf16[512]{0:T(512)(128)(2,1)} %param.26) | copy-start | bytes 3076
  89.5 15.0 %all-to-all-start.2 = ((bf16[8,512,72]{1,2,0:T(8,128)(2,1)}), bf16[8,512,72]{1,2,0:T(8,128)(2,1)S(1)}, u32[]{:S(2)}, u32[]{:S(2)}) async-start(bf16[8,512,72]{1,2,0:T(8,128)(2,1)} %broadcast_in_dim.56), calls=%async_computation.2 | async-start | bytes 1179648 | tf_op jit(solution)/shard_map/all_to_all | solution.py:73
  106.2 14.8 %all-to-all-start.1 = ((bf16[4,256,192]{1,2,0:T(8,128)(2,1)}), bf16[4,256,192]{1,2,0:T(8,128)(2,1)S(1)}, u32[]{:S(2)}, u32[]{:S(2)}) async-start(bf16[4,256,192]{1,2,0:T(8,128)(2,1)} %bitcast.13), calls=%async_computation.1 | async-start | bytes 786432 | tf_op jit(solution)/shard_map/all_to_all | solution.py:73
  122.8 54.2 %all-to-all-start.3 = ((bf16[16,256,320]{1,2,0:T(8,128)(2,1)}), bf16[16,256,320]{1,2,0:T(8,128)(2,1)S(1)}, u32[]{:S(2)}, u32[]{:S(2)}) async-start(bf16[16,256,320]{1,2,0:T(8,128)(2,1)} %bitcast.163), calls=%async_computation.3 | async-start | bytes 5242880 | tf_op jit(solution)/shard_map/all_to_all | solution.py:73
  213.7 35.7 %all-to-all-start.5 = ((bf16[8,64,2048]{2,1,0:T(8,128)(2,1)}), bf16[8,64,2048]{2,1,0:T(8,128)(2,1)S(1)}, u32[]{:S(2)}, u32[]{:S(2)}) async-start(bf16[8,64,2048]{2,1,0:T(8,128)(2,1)} %bitcast.164), calls=%async_computation.5 | async-start | bytes 4194304 | tf_op jit(solution)/shard_map/all_to_all | solution.py:73
  251.4 33.0 %all-to-all-start.7 = ((bf16[8,512,256]{1,2,0:T(8,128)(2,1)}), bf16[8,512,256]{1,2,0:T(8,128)(2,1)S(1)}, u32[]{:S(2)}, u32[]{:S(2)}) async-start(bf16[8,512,256]{1,2,0:T(8,128)(2,1)} %broadcast_in_dim.62), calls=%async_computation.7 | async-start | bytes 4194304 | tf_op jit(solution)/shard_map/all_to_all | solution.py:73
  260.1 155.7 %copy-start.62 = (f32[64]{0:T(128)}, f32[64]{0:T(128)S(1)}, u32[]{:S(2)}) copy-start(f32[64]{0:T(128)S(1)} %get-tuple-element.157) | copy-start | bytes 772
  260.1 155.7 %copy-start.68 = (f32[64]{0:T(128)}, f32[64]{0:T(128)S(1)}, u32[]{:S(2)}) copy-start(f32[64]{0:T(128)S(1)} %get-tuple-element.156) | copy-start | bytes 772
  287.0 32.8 %all-to-all-start.6 = ((bf16[8,64,2048]{2,1,0:T(8,128)(2,1)}), bf16[8,64,2048]{2,1,0:T(8,128)(2,1)S(1)}, u32[]{:S(2)}, u32[]{:S(2)}) async-start(bf16[8,64,2048]{2,1,0:T(8,128)(2,1)} %broadcast_in_dim.60), calls=%async_computation.6 | async-start | bytes 4194304 | tf_op jit(solution)/shard_map/all_to_all | solution.py:73
  290.8 464.3 %reduce-scatter.2.cloned.1.call-start = ((), (), s32[]{:S(2)}) async-start(), calls=%async_computation.22 | async-start | bytes 23396352 | tf_op jit(solution)/shard_map/reduce_scatter | solution.py:501
  418.5 30.8 %copy-start.26 = (bf16[2048,896]{0,1:T(8,128)(2,1)S(1)}, bf16[2048,896]{0,1:T(8,128)(2,1)}, u32[]{:S(2)}) copy-start(bf16[2048,896]{0,1:T(8,128)(2,1)} %all-gather.3.cloned.1.call-done) | copy-start | bytes 11010052
  450.9 16.8 %all-to-all-start.11 = ((bf16[4,256,128]{2,1,0:T(8,128)(2,1)}), bf16[4,256,128]{2,1,0:T(8,128)(2,1)}, u32[]{:S(2)}, u32[]{:S(2)}) async-start(bf16[4,256,128]{2,1,0:T(8,128)(2,1)} %bitcast.43), calls=%async_computation.11 | async-start | bytes 524288 | tf_op jit(solution)/shard_map/all_to_all | solution.py:73
  486.5 13.4 %all-to-all-start.12 = ((bf16[4,256,192]{1,2,0:T(8,128)(2,1)}), bf16[4,256,192]{1,2,0:T(8,128)(2,1)S(1)}, u32[]{:S(2)}, u32[]{:S(2)}) async-start(bf16[4,256,192]{1,2,0:T(8,128)(2,1)} %copy.303), calls=%async_computation.12 | async-start | bytes 786432 | tf_op jit(solution)/shard_map/all_to_all | solution.py:73
  499.9 44.8 %all-to-all-start.13 = ((bf16[16,256,320]{1,2,0:T(8,128)(2,1)}), bf16[16,256,320]{1,2,0:T(8,128)(2,1)}, u32[]{:S(2)}, u32[]{:S(2)}) async-start(bf16[16,256,320]{1,2,0:T(8,128)(2,1)} %copy.305), calls=%async_computation.13 | async-start | bytes 5242880 | tf_op jit(solution)/shard_map/all_to_all | solution.py:73
  557.6 16.0 %all-to-all-start.14 = ((bf16[8,512,72]{1,2,0:T(8,128)(2,1)}), bf16[8,512,72]{1,2,0:T(8,128)(2,1)}, u32[]{:S(2)}, u32[]{:S(2)}) async-start(bf16[8,512,72]{1,2,0:T(8,128)(2,1)} %bitcast.172), calls=%async_computation.14 | async-start | bytes 1179648 | tf_op jit(solution)/shard_map/all_to_all | solution.py:73
  582.6 18.1 %all-to-all-start.16 = ((f32[128,1,36]{2,1,0:T(1,128)}), f32[128,1,36]{2,1,0:T(1,128)S(1)}, u32[]{:S(2)}, u32[]{:S(2)}) async-start(f32[128,1,36]{2,1,0:T(1,128)} %bitcast.209), calls=%async_computation.16 | async-start | bytes 131072 | tf_op jit(solution)/shard_map/all_to_all | solution.py:73
  600.7 35.3 %all-to-all-start.8 = ((bf16[8,512,256]{2,1,0:T(8,128)(2,1)}), bf16[8,512,256]{2,1,0:T(8,128)(2,1)}, u32[]{:S(2)}, u32[]{:S(2)}) async-start(bf16[8,512,256]{2,1,0:T(8,128)(2,1)} %fusion.23), calls=%async_computation.8 | async-start | bytes 4194304 | tf_op jit(solution)/shard_map/all_to_all | solution.py:73
  637.3 17.9 %all-to-all-start.17 = ((f32[128,1,36]{2,1,0:T(1,128)}), f32[128,1,36]{2,1,0:T(1,128)S(1)}, u32[]{:S(2)}, u32[]{:S(2)}) async-start(f32[128,1,36]{2,1,0:T(1,128)} %broadcast_in_dim.125), calls=%async_computation.17 | async-start | bytes 131072 | tf_op jit(solution)/shard_map/all_to_all | solution.py:73
  655.2 37.9 %all-to-all-start.15 = ((bf16[8,512,256]{1,2,0:T(8,128)(2,1)}), bf16[8,512,256]{1,2,0:T(8,128)(2,1)}, u32[]{:S(2)}, u32[]{:S(2)}) async-start(bf16[8,512,256]{1,2,0:T(8,128)(2,1)} %bitcast.54), calls=%async_computation.15 | async-start | bytes 4194304 | tf_op jit(solution)/shard_map/all_to_all | solution.py:73
  693.1 56.2 %all-to-all-start.18 = ((bf16[16,128,896]{2,1,0:T(8,128)(2,1)}), bf16[16,128,896]{2,1,0:T(8,128)(2,1)}, u32[]{:S(2)}, u32[]{:S(2)}) async-start(bf16[16,128,896]{2,1,0:T(8,128)(2,1)} %concatenate.102), calls=%async_computation.18 | async-start | bytes 7340032 | tf_op jit(solution)/shard_map/all_to_all | solution.py:73
  (69 other events, 394.9 us)
Sparse Core Ops, SparseCore 0:
  11.8 74.5 all-gather.2
  88.8 170.0 all-gather.4
  363.8 236.4 reduce-scatter.1

commit v2 on v1

v2 whole, which is shorter than its diff:
```python
import functools

import jax
import jax.numpy as jnp
from jax import lax
from jax.experimental import pallas as pl
from jax.experimental.pallas import tpu as pltpu
from jax.sharding import PartitionSpec as P

D = 2048
NOPE = 128
ROPE = 64
QK = NOPE + ROPE
VDIM = 128
KVL = 512
TOPK = 6
EXPERTS = 8
MICRO = 2
TRUNK = 1024
BLK = 256
SEGS = 13
ROWS = 16
COLS = 8
TOK = MICRO * BLK
OWN = TOK // COLS
FEAT = D // COLS
QUART = 4
SHARED = 352
ROUTED = 176
HID = 1792
LAT = KVL + ROPE
HALF = BLK // 2
QKP = 256
PACK = VDIM + QKP
WIDE = 3 * HID
CUT = WIDE // 2
LANES = D // ROWS
LATC = LAT // COLS
SCALE = QK**-0.5
EPS = 1e-06
THETA = 10000.0
NEG = -1e30
MIB = 1024 * 1024
F32 = jnp.float32
BF16 = jnp.bfloat16
NT = (((1,), (1,)), ((), ()))
TN = (((0,), (0,)), ((), ()))


def inverse_rms(values):
    return lax.rsqrt(jnp.mean(values * values, axis=-1, keepdims=True) + EPS)


def norm_backward(grad_out, values, inv_scale, norm_gain):
    weighted = grad_out * norm_gain
    inner = jnp.mean(weighted * values, axis=-1, keepdims=True)
    return inv_scale * weighted - values * (inv_scale * inv_scale * inv_scale) * inner


def matmul(a, b):
    return jnp.dot(a, b, preferred_element_type=F32)


def matmul_nt(a, b):
    return lax.dot_general(a, b, NT, preferred_element_type=F32)


def matmul_tn(a, b):
    return lax.dot_general(a, b, TN, preferred_element_type=F32)


def swap(values, axis, groups=None):
    return lax.all_to_all(values, axis, 0, 0, tiled=True, axis_index_groups=groups)


def share(values, axis, count):
    return swap(jnp.broadcast_to(values[None], (count,) + values.shape), axis)


def trade(values, axis, mask):
    count = ROWS if axis == "row" else COLS
    return lax.ppermute(values, axis, [(i, i ^ mask) for i in range(count)])


def after(values, *others):
    return lax.optimization_barrier((values,) + others)[0]


def together(*values):
    return lax.optimization_barrier(values)


def smem_values(*values):
    return jnp.stack([jnp.asarray(v, jnp.int32) for v in values])


def pick(values, index, axis=0):
    return lax.dynamic_index_in_dim(values, index, axis, keepdims=False)


def pair_up(shard, axis):
    return jnp.stack([shard, trade(shard, axis, 8 if axis == "row" else 1)])


def ring_up(pair, axis):
    return [pair] + [trade(pair, axis, j << 1) for j in (1, 2, 3)]


def sort_rows_kernel(own_ref, near_ref, far_ref, out_ref):
    for core, ref in ((0, near_ref), (1, far_ref)):
        for x in range(4):
            for z in range(2):
                out_ref[own_ref[0] ^ (8 * z + 2 * x + core)] = ref[x, z]


def finish_rows(ring, row):
    near = jnp.stack(ring)
    far = trade(near, "row", 1)
    vmem = pl.BlockSpec(memory_space=pltpu.VMEM)
    out = pl.pallas_call(
        sort_rows_kernel,
        out_shape=jax.ShapeDtypeStruct((ROWS,) + near.shape[2:], near.dtype),
        in_specs=[pl.BlockSpec(memory_space=pltpu.SMEM), vmem, vmem],
        out_specs=vmem,
        compiler_params=pltpu.CompilerParams(vmem_limit_bytes=16 * MIB),
        cost_estimate=pl.CostEstimate(flops=0, bytes_accessed=near.size, transcendentals=0),
    )(smem_values(row), near, far)
    return out.reshape(D, near.shape[3])


def place_of(apart):
    return ((apart & 1) << 3) | ((apart >> 3) << 2) | ((apart >> 1) & 3)


def lanes(at):
    return pl.ds(pl.multiple_of(at * LANES, LANES), LANES)


def features_kernel(own_ref, blocks_ref, out_ref, out_t_ref):
    for c in range(COLS):
        out_ref[:, c * FEAT : (c + 1) * FEAT] = blocks_ref[c]
    for r in range(ROWS):
        block = blocks_ref[r // 2, :, (r % 2) * LANES : (r % 2 + 1) * LANES]
        out_t_ref[lanes(place_of(own_ref[0] ^ r)), :] = block.T


def features(row, blocks):
    vmem = pl.BlockSpec(memory_space=pltpu.VMEM)
    return pl.pallas_call(
        features_kernel,
        out_shape=(
            jax.ShapeDtypeStruct((TOK, D), BF16),
            jax.ShapeDtypeStruct((D, TOK), BF16),
        ),
        in_specs=[pl.BlockSpec(memory_space=pltpu.SMEM), vmem],
        out_specs=(vmem, vmem),
        compiler_params=pltpu.CompilerParams(vmem_limit_bytes=60 * MIB),
        cost_estimate=pl.CostEstimate(flops=0, bytes_accessed=MIB, transcendentals=0),
    )(smem_values(row), blocks)


def turn_kernel(own_ref, x_ref, out_ref):
    for r in range(ROWS):
        block = x_ref[:, r * LANES : (r + 1) * LANES]
        out_ref[lanes(place_of(own_ref[0] ^ r)), :] = block.T


def turn(row, values):
    vmem = pl.BlockSpec(memory_space=pltpu.VMEM)
    return pl.pallas_call(
        turn_kernel,
        out_shape=jax.ShapeDtypeStruct((D, TOK), BF16),
        in_specs=[pl.BlockSpec(memory_space=pltpu.SMEM), vmem],
        out_specs=vmem,
        compiler_params=pltpu.CompilerParams(vmem_limit_bytes=60 * MIB),
        cost_estimate=pl.CostEstimate(flops=0, bytes_accessed=MIB, transcendentals=0),
    )(smem_values(row), values)


def near_shards(shard):
    return trade(shard, "row", 2), trade(shard, "row", 6)


def far_halves(near):
    return trade(near[1][:, :CUT], "row", 2), trade(near[0][:, CUT:], "row", 6)


def put_kernel(places, own_ref, *refs):
    out_ref, sems = refs[-2:]
    copies = []
    for i, (apart, first) in enumerate(places):
        rows = lanes(own_ref[0] ^ apart)
        columns = pl.ds(first, refs[i].shape[1])
        copy = pltpu.make_async_copy(refs[i], out_ref.at[rows, columns], sems.at[i])
        copy.start()
        copies.append(copy)
    for copy in copies:
        copy.wait()


def put_shards(row, whole, pieces):
    values = [piece for piece, _, _ in pieces]
    places = [(apart, first) for _, apart, first in pieces]
    fresh = whole is None
    return pl.pallas_call(
        functools.partial(put_kernel, places),
        out_shape=jax.ShapeDtypeStruct((D, WIDE), BF16),
        in_specs=[pl.BlockSpec(memory_space=pltpu.SMEM)]
        + [pl.BlockSpec(memory_space=pltpu.VMEM)] * len(values)
        + ([] if fresh else [pl.BlockSpec(memory_space=pl.ANY)]),
        out_specs=pl.BlockSpec(memory_space=pl.ANY),
        scratch_shapes=[pltpu.SemaphoreType.DMA((len(values),))],
        input_output_aliases={} if fresh else {1 + len(values): 0},
        compiler_params=pltpu.CompilerParams(vmem_limit_bytes=60 * MIB),
        cost_estimate=pl.CostEstimate(flops=0, bytes_accessed=MIB, transcendentals=0),
    )(smem_values(row), *values, *([] if fresh else [whole]))


def sum_opposite(blocks):
    return trade(blocks[2][:, :CUT], "row", 2), trade(blocks[2][:, CUT:], "row", 6)


def add_low(a, b):
    return (a.astype(F32) + b.astype(F32)).astype(BF16)


def sides_kernel(b1_ref, b3_ref, h1_ref, h3_ref, left_ref, right_ref):
    left_ref[:, :CUT] = b1_ref[:, :CUT]
    left_ref[:, CUT:] = (b1_ref[:, CUT:].astype(F32) + h3_ref[...].astype(F32)).astype(BF16)
    right_ref[:, :CUT] = (b3_ref[:, :CUT].astype(F32) + h1_ref[...].astype(F32)).astype(BF16)
    right_ref[:, CUT:] = b3_ref[:, CUT:]


def with_opposite(blocks, halves):
    return pl.pallas_call(
        sides_kernel,
        out_shape=[jax.ShapeDtypeStruct((LANES, WIDE), BF16)] * 2,
        compiler_params=pltpu.CompilerParams(vmem_limit_bytes=60 * MIB),
        cost_estimate=pl.CostEstimate(flops=0, bytes_accessed=MIB, transcendentals=0),
    )(blocks[1], blocks[3], *halves)


def sum_neighbours(sides):
    return trade(sides[0], "row", 2), trade(sides[1], "row", 6)


def reduce_row(keep, send):
    shape = (4, 2) + keep.shape[1:]
    blocks = add_low(keep, trade(send, "row", 1)).reshape(shape)
    got = [trade(blocks[j], "row", j << 1).astype(F32) for j in (1, 2, 3)]
    blocks = (blocks[0].astype(F32) + got[0] + got[1] + got[2]).astype(BF16)
    return blocks[0].astype(F32) + trade(blocks[1], "row", 8).astype(F32)


def attn_grads_kernel(
    own_ref, x_ref, dq_ref, dl_ref, low_ref, att_ref, lat_ref, de_ref, keep_ref, send_ref, out
):
    out[:, :384] = matmul_tn(x_ref[...], dq_ref[...])
    out[:, 384:640] = matmul_tn(low_ref[...], att_ref[...])
    expand_grad = matmul(lat_ref[...], de_ref[...])
    for half in range(2):
        for i in range(4):
            rows = slice(half * LANES + 32 * i, half * LANES + 32 * (i + 1))
            part = expand_grad[32 * half : 32 * (half + 1), 128 * i : 128 * (i + 1)]
            out[rows, 640:768] = part
    out[:, 768:] = matmul_tn(x_ref[...], dl_ref[...])
    core = own_ref[0] & 1
    keep_ref[0] = out[lanes(core), :].astype(BF16)
    send_ref[0] = out[lanes(1 - core), :].astype(BF16)


def attn_weight_grads(row, normed, d_query, d_latent, d_low, attended, latent_t, d_expanded):
    def whole(shape):
        return pl.BlockSpec(shape, lambda i, own: (0, 0))

    def place(i, own):
        apart = i ^ (own[0] >> 1)
        return (apart & 3) * 2 + (apart >> 2), 0, 0

    columns = pl.BlockSpec((TOK, 2 * LANES), lambda i, own: (0, i))
    block = pl.BlockSpec((1, LANES, 896), place)
    return pl.pallas_call(
        attn_grads_kernel,
        out_shape=[jax.ShapeDtypeStruct((ROWS // 2, LANES, 896), BF16)] * 2,
        grid_spec=pltpu.PrefetchScalarGridSpec(
            num_scalar_prefetch=1,
            grid=(ROWS // 2,),
            in_specs=[
                columns,
                whole(d_query.shape),
                whole(d_latent.shape),
                columns,
                whole(attended.shape),
                pl.BlockSpec((2 * KVL // ROWS, TOK), lambda i, own: (i, 0)),
                whole(d_expanded.shape),
            ],
            out_specs=[block, block],
            scratch_shapes=[pltpu.VMEM((2 * LANES, 896), F32)],
        ),
        compiler_params=pltpu.CompilerParams(vmem_limit_bytes=60 * MIB),
        cost_estimate=pl.CostEstimate(flops=TOK * D * 64, bytes_accessed=MIB, transcendentals=0),
    )(smem_values(row), normed, d_query, d_latent, d_low, attended, latent_t, d_expanded)


def collect_y(blocks, y):
    blocks = blocks.reshape((4, 2) + blocks.shape[1:])
    return [pick(blocks, y)] + [trade(pick(blocks, y ^ j), "col", j << 1) for j in (1, 2, 3)]


def collect_z(blocks, z):
    blocks = [block.astype(F32) for block in blocks]
    blocks = (blocks[0] + blocks[1] + (blocks[2] + blocks[3])).astype(BF16)
    got = trade(pick(blocks, 1 - z), "col", 1)
    return pick(blocks, z).astype(F32) + got.astype(F32)


def trade_quarter(blocks):
    return [blocks[0]] + [trade(blocks[j], "row", j << 2) for j in (1, 2, 3)]


def depth_kernel(parents_ref, seg_ref, out_ref):
    seg = seg_ref[0]
    for m in range(MICRO):

        def climb(step, state):
            at, count = state
            return parents_ref[m, at], count + (at > 0).astype(jnp.int32)

        _, count = lax.fori_loop(0, SEGS, climb, (parents_ref[m, seg], jnp.int32(0)))
        out_ref[m] = count


def ancestor_depths(parents, seg):
    smem = pl.BlockSpec(memory_space=pltpu.SMEM)
    return pl.pallas_call(
        depth_kernel,
        out_shape=jax.ShapeDtypeStruct((MICRO,), jnp.int32),
        in_specs=[smem, smem],
        out_specs=smem,
    )(parents, seg)


def list_ancestors(meta, qb, listed):
    def climb(step, state):
        at, count = state
        listed[count] = at + 3
        return meta[at], count + (at > 0).astype(jnp.int32)

    _, count = lax.fori_loop(0, SEGS, climb, (meta[qb - 3], jnp.int32(0)))
    return count


def causal_mask():
    key = lax.broadcasted_iota(jnp.int32, (BLK, BLK), 0)
    query = lax.broadcasted_iota(jnp.int32, (BLK, BLK), 1)
    return key <= query


def join_halves(meta, near_ref, far_ref, pack):
    core = meta[SEGS] % 2
    pack[:, pl.ds(pl.multiple_of(core * HALF, HALF), HALF), :] = near_ref[...]
    pack[:, pl.ds(pl.multiple_of((1 - core) * HALF, HALF), HALF), :] = far_ref[...]


def attend_kernel(meta, q0, q1, q2, q3, near_ref, far_ref, o0, o1, o2, o3, lse_ref, *scratch):
    q_ref, o_ref, pack, listed = scratch
    quarter, own = meta[SEGS], meta[SEGS + 1]
    join_halves(meta, near_ref, far_ref, pack)
    for j, ref in enumerate((q0, q1, q2, q3)):
        q_ref[own ^ j] = ref[...]
    for i in range(QUART):
        qb = QUART * i + quarter
        q = q_ref[i]
        s = matmul_nt(pack[qb, :, VDIM:], q) * SCALE
        s = jnp.where(causal_mask(), s, NEG)
        top = jnp.max(s, axis=0, keepdims=True)
        p = jnp.exp(s - top)
        total = jnp.sum(p, axis=0, keepdims=True)
        out = matmul_tn(pack[qb, :, :VDIM], p.astype(BF16))

        def step(kb, state):
            top, total, out = state
            s = matmul_nt(pack[kb, :, VDIM:], q) * SCALE
            new_top = jnp.maximum(top, jnp.max(s, axis=0, keepdims=True))
            shrink = jnp.exp(top - new_top)
            p = jnp.exp(s - new_top)
            total = total * shrink + jnp.sum(p, axis=0, keepdims=True)
            out = out * shrink + matmul_tn(pack[kb, :, :VDIM], p.astype(BF16))
            return new_top, total, out

        state = (top, total, out)
        if i == 0:
            state = lax.fori_loop(0, quarter, step, state)
        else:
            for kb in range(TRUNK // BLK):
                state = step(kb, state)
            count = list_ancestors(meta, qb, listed)
            state = lax.fori_loop(0, count, lambda t, c: step(listed[t], c), state)
        top, total, out = state
        o_ref[i] = (out * (1.0 / total)).T.astype(BF16)
        lse_ref[i] = top + jnp.log(total)
    for j, ref in enumerate((o0, o1, o2, o3)):
        ref[...] = o_ref[own ^ j]


def attend(meta, q, near, far):
    smem = pl.BlockSpec(memory_space=pltpu.SMEM)
    vmem = pl.BlockSpec(memory_space=pltpu.VMEM)
    pairs = 32 * BLK * BLK
    return pl.pallas_call(
        attend_kernel,
        out_shape=[jax.ShapeDtypeStruct((BLK, VDIM), BF16)] * QUART
        + [jax.ShapeDtypeStruct((QUART, 1, BLK), F32)],
        in_specs=[smem] + [vmem] * 6,
        out_specs=[vmem] * 5,
        scratch_shapes=[
            pltpu.VMEM((QUART, BLK, QKP), BF16),
            pltpu.VMEM((QUART, BLK, VDIM), BF16),
            pltpu.VMEM((ROWS, BLK, PACK), BF16),
            pltpu.SMEM((16,), jnp.int32),
        ],
        compiler_params=pltpu.CompilerParams(vmem_limit_bytes=60 * MIB),
        cost_estimate=pl.CostEstimate(
            flops=pairs * 2 * (QK + VDIM), bytes_accessed=4 * MIB, transcendentals=pairs
        ),
    )(meta, *q, near, far)


def attend_back_kernel(meta, *refs):
    ins, outs, scratch = refs[:15], refs[15:21], refs[21:]
    near_ref, far_ref, lse_ref = ins[12:]
    keep_ref, send_ref = outs[4:]
    q_ref, o_ref, do_ref, dq_ref, pack, dk, dv, listed = scratch
    quarter, own = meta[SEGS], meta[SEGS + 1]
    core = quarter % 2
    join_halves(meta, near_ref, far_ref, pack)
    for j in range(QUART):
        q_ref[own ^ j] = ins[j][...]
        o_ref[own ^ j] = ins[QUART + j][...]
        do_ref[own ^ j] = ins[2 * QUART + j][...]
    dk[...] = jnp.zeros_like(dk)
    dv[...] = jnp.zeros_like(dv)
    for i in range(QUART):
        qb = QUART * i + quarter
        q = q_ref[i]
        do = do_ref[i]
        lse = lse_ref[i]
        pairs = do.astype(F32) * o_ref[i].astype(F32)
        delta = jnp.sum(pairs.T, axis=0, keepdims=True)

        def step(kb, dqt, masked=False):
            key = pack[kb, :, VDIM:]
            s = matmul_nt(key, q) * SCALE
            p = jnp.exp(s - lse)
            if masked:
                p = jnp.where(causal_mask(), p, 0.0)
            dp = matmul_nt(pack[kb, :, :VDIM], do)
            ds = (p * (dp - delta) * SCALE).astype(BF16)
            dv[kb] += matmul(p.astype(BF16), do)
            dk[kb] += matmul(ds, q)
            return dqt + matmul_tn(key, ds)

        dqt = step(qb, jnp.zeros((QKP, BLK), F32), True)
        if i == 0:
            dqt = lax.fori_loop(0, quarter, step, dqt)
        else:
            for kb in range(TRUNK // BLK):
                dqt = step(kb, dqt)
            count = list_ancestors(meta, qb, listed)
            dqt = lax.fori_loop(0, count, lambda t, c: step(listed[t], c), dqt)
        dq_ref[i] = dqt.T.astype(BF16)
    for j in range(QUART):
        outs[j][...] = dq_ref[own ^ j]
    for half, ref in ((core, keep_ref), (1 - core, send_ref)):
        part = pl.ds(pl.multiple_of(half * HALF, HALF), HALF)
        ref[:, :, :VDIM] = dv[:, part, :].astype(BF16)
        ref[:, :, VDIM:] = dk[:, part, :].astype(BF16)


def attend_back(meta, q, o, d_o, near, far, lse):
    smem = pl.BlockSpec(memory_space=pltpu.SMEM)
    vmem = pl.BlockSpec(memory_space=pltpu.VMEM)
    pairs = 32 * BLK * BLK
    return pl.pallas_call(
        attend_back_kernel,
        out_shape=[jax.ShapeDtypeStruct((BLK, QKP), BF16)] * QUART
        + [jax.ShapeDtypeStruct((ROWS, HALF, PACK), BF16)] * 2,
        in_specs=[smem] + [vmem] * 15,
        out_specs=[vmem] * 6,
        scratch_shapes=[
            pltpu.VMEM((QUART, BLK, QKP), BF16),
            pltpu.VMEM((QUART, BLK, VDIM), BF16),
            pltpu.VMEM((QUART, BLK, VDIM), BF16),
            pltpu.VMEM((QUART, BLK, QKP), BF16),
            pltpu.VMEM((ROWS, BLK, PACK), BF16),
            pltpu.VMEM((ROWS, BLK, QKP), F32),
            pltpu.VMEM((ROWS, BLK, VDIM), F32),
            pltpu.SMEM((16,), jnp.int32),
        ],
        compiler_params=pltpu.CompilerParams(vmem_limit_bytes=60 * MIB),
        cost_estimate=pl.CostEstimate(
            flops=pairs * 2 * (3 * QK + 2 * VDIM), bytes_accessed=10 * MIB, transcendentals=pairs
        ),
    )(meta, *q, *o, *d_o, near, far, lse)


def project_kernel(own_ref, b0, b1, b2, b3, w_ref, attended_ref, out_ref, blocks):
    for j, ref in enumerate((b0, b1, b2, b3)):
        blocks[own_ref[0] ^ j] = ref[...]
    for h in range(2):
        for m in range(MICRO):
            attended_ref[m * BLK : (m + 1) * BLK, h * VDIM : (h + 1) * VDIM] = blocks[2 * h + m]
    out = matmul_nt(attended_ref[...], w_ref[...]).astype(BF16)
    for c in range(COLS):
        out_ref[c] = out[c * OWN : (c + 1) * OWN]


def project(own, blocks, w_output):
    vmem = pl.BlockSpec(memory_space=pltpu.VMEM)
    return pl.pallas_call(
        project_kernel,
        out_shape=(
            jax.ShapeDtypeStruct((TOK, 2 * VDIM), BF16),
            jax.ShapeDtypeStruct((COLS, OWN, D), BF16),
        ),
        in_specs=[pl.BlockSpec(memory_space=pltpu.SMEM)] + [vmem] * 5,
        out_specs=(vmem, vmem),
        scratch_shapes=[pltpu.VMEM((QUART, BLK, VDIM), BF16)],
        compiler_params=pltpu.CompilerParams(vmem_limit_bytes=60 * MIB),
        cost_estimate=pl.CostEstimate(flops=TOK * D * 512, bytes_accessed=MIB, transcendentals=0),
    )(smem_values(own), *blocks, w_output)


def project_back_kernel(own_ref, d_ref, w_ref, o0, o1, o2, o3, blocks):
    for c in range(COLS):
        rows = slice((c % QUART) * OWN, (c % QUART + 1) * OWN)
        part = matmul(d_ref[c], w_ref[...]).astype(BF16)
        for h in range(2):
            blocks[2 * h + c // QUART, rows, :] = part[:, h * VDIM : (h + 1) * VDIM]
    for j, ref in enumerate((o0, o1, o2, o3)):
        ref[...] = blocks[own_ref[0] ^ j]


def project_back(own, d_low, w_output):
    vmem = pl.BlockSpec(memory_space=pltpu.VMEM)
    return pl.pallas_call(
        project_back_kernel,
        out_shape=[jax.ShapeDtypeStruct((BLK, VDIM), BF16)] * QUART,
        in_specs=[pl.BlockSpec(memory_space=pltpu.SMEM)] + [vmem] * 2,
        out_specs=[vmem] * QUART,
        scratch_shapes=[pltpu.VMEM((QUART, BLK, VDIM), BF16)],
        compiler_params=pltpu.CompilerParams(vmem_limit_bytes=60 * MIB),
        cost_estimate=pl.CostEstimate(flops=TOK * D * 512, bytes_accessed=MIB, transcendentals=0),
    )(smem_values(own), d_low, w_output)


def front_kernel(col_ref, p0, p1, p2, p3, gain_ref, wl_ref, x_ref, normed_ref, scale_ref, lat_ref):
    for y, ref in enumerate((p0, p1, p2, p3)):
        for z in range(2):
            at = (col_ref[0] ^ (2 * y + z)) * FEAT
            x_ref[:, pl.ds(pl.multiple_of(at, FEAT), FEAT)] = ref[z]
    x = x_ref[...].astype(F32)
    scale = inverse_rms(x)
    scale_ref[...] = scale
    normed = (x * scale * gain_ref[...]).astype(BF16)
    normed_ref[...] = normed
    latent = matmul(normed, wl_ref[...]).T[:LATC].astype(BF16)
    for c in range(COLS):
        lat_ref[c] = latent


def front(col, ring, gain, w_latent):
    rows = 128
    return pl.pallas_call(
        front_kernel,
        grid=(TOK // rows,),
        out_shape=(
            jax.ShapeDtypeStruct((TOK, D), BF16),
            jax.ShapeDtypeStruct((TOK, D), BF16),
            jax.ShapeDtypeStruct((TOK, 1), F32),
            jax.ShapeDtypeStruct((COLS, LATC, TOK), BF16),
        ),
        in_specs=[pl.BlockSpec(memory_space=pltpu.SMEM)]
        + [pl.BlockSpec((2, rows, FEAT), lambda j: (0, j, 0))] * 4
        + [
            pl.BlockSpec((1, D), lambda j: (0, 0)),
            pl.BlockSpec((D, 128), lambda j: (0, 0)),
        ],
        out_specs=(
            pl.BlockSpec((rows, D), lambda j: (j, 0)),
            pl.BlockSpec((rows, D), lambda j: (j, 0)),
            pl.BlockSpec((rows, 1), lambda j: (j, 0)),
            pl.BlockSpec((COLS, LATC, rows), lambda j: (0, 0, j)),
        ),
        compiler_params=pltpu.CompilerParams(vmem_limit_bytes=60 * MIB),
        cost_estimate=pl.CostEstimate(flops=TOK * D * 256, bytes_accessed=MIB, transcendentals=0),
    )(smem_values(col), *ring, gain.reshape(1, D), w_latent)


def half_turn():
    source = lax.broadcasted_iota(jnp.int32, (2 * ROPE, 2 * ROPE), 0)
    target = lax.broadcasted_iota(jnp.int32, (2 * ROPE, 2 * ROPE), 1)
    half = ROPE // 2
    first = target % ROPE < half
    value = jnp.where(
        first & (source == target + half),
        -1.0,
        jnp.where((target % ROPE >= half) & (source == target - half), 1.0, 0.0),
    )
    return value.astype(BF16)


def query_kernel(own_ref, normed_ref, w_ref, cos_ref, sin_ref, o0, o1, o2, o3, blocks):
    normed = normed_ref[...]
    w_rope = w_ref[:, 2 * NOPE :]
    turned = matmul(w_rope, half_turn()).astype(BF16)
    rope = matmul(normed, w_rope) * cos_ref[...] + matmul(normed, turned) * sin_ref[...]
    rope = rope.astype(BF16)
    nope = matmul(normed, w_ref[:, : 2 * NOPE]).astype(BF16)
    blank = jnp.zeros((BLK, QKP - QK), BF16)
    for h in range(2):
        for m in range(MICRO):
            rows = slice(m * BLK, (m + 1) * BLK)
            blocks[2 * h + m, :, :NOPE] = nope[rows, h * NOPE : (h + 1) * NOPE]
            blocks[2 * h + m, :, NOPE:QK] = rope[rows, h * ROPE : (h + 1) * ROPE]
            blocks[2 * h + m, :, QK:] = blank
    for j, ref in enumerate((o0, o1, o2, o3)):
        ref[...] = blocks[own_ref[0] ^ j]


def project_query(own, normed, w_query, cos_wide, sin_wide):
    vmem = pl.BlockSpec(memory_space=pltpu.VMEM)
    return pl.pallas_call(
        query_kernel,
        out_shape=[jax.ShapeDtypeStruct((BLK, QKP), BF16)] * QUART,
        in_specs=[pl.BlockSpec(memory_space=pltpu.SMEM)] + [vmem] * 4,
        out_specs=[vmem] * QUART,
        scratch_shapes=[pltpu.VMEM((QUART, BLK, QKP), BF16)],
        compiler_params=pltpu.CompilerParams(vmem_limit_bytes=60 * MIB),
        cost_estimate=pl.CostEstimate(flops=TOK * D * 256, bytes_accessed=MIB, transcendentals=0),
    )(smem_values(own), normed, w_query, cos_wide, sin_wide)


def query_back_kernel(own_ref, b0, b1, b2, b3, cos_ref, sin_ref, out_ref, blocks):
    turn = half_turn()
    for j, ref in enumerate((b0, b1, b2, b3)):
        blocks[own_ref[0] ^ j] = ref[...]
    for m in range(MICRO):
        rows = slice(m * BLK, (m + 1) * BLK)
        for h in range(2):
            out_ref[rows, h * NOPE : (h + 1) * NOPE] = blocks[2 * h + m, :, :NOPE]
        rope = jnp.concatenate([blocks[m, :, NOPE:QK], blocks[2 + m, :, NOPE:QK]], axis=1)
        rope = rope.astype(F32) * cos_ref[rows, :] + matmul_nt(rope, turn) * sin_ref[rows, :]
        out_ref[rows, 2 * NOPE :] = rope.astype(BF16)


def query_back(own, blocks, cos_wide, sin_wide):
    vmem = pl.BlockSpec(memory_space=pltpu.VMEM)
    return pl.pallas_call(
        query_back_kernel,
        out_shape=jax.ShapeDtypeStruct((TOK, 2 * QK), BF16),
        in_specs=[pl.BlockSpec(memory_space=pltpu.SMEM)] + [vmem] * 6,
        out_specs=vmem,
        scratch_shapes=[pltpu.VMEM((QUART, BLK, QKP), BF16)],
        compiler_params=pltpu.CompilerParams(vmem_limit_bytes=60 * MIB),
        cost_estimate=pl.CostEstimate(flops=TOK * D * 16, bytes_accessed=MIB, transcendentals=0),
    )(smem_values(own), *blocks, cos_wide, sin_wide)


def expand_kernel(latent_ref, cos_ref, sin_ref, gain_ref, w_ref, normed_ref, out_ref):
    c = latent_ref[:KVL, :].astype(F32)
    scale = lax.rsqrt(jnp.mean(c * c, axis=0, keepdims=True) + EPS)
    normed = (c * scale * gain_ref[...]).astype(BF16)
    normed_ref[...] = normed
    expanded = matmul_tn(normed, w_ref[...]).astype(BF16)
    half = ROPE // 2
    a = latent_ref[KVL : KVL + half, :].astype(F32)
    b = latent_ref[KVL + half :, :].astype(F32)
    cos, sin = cos_ref[...], sin_ref[...]
    rope = jnp.concatenate(
        [a * cos - b * sin, a * sin + b * cos, jnp.zeros((QKP - QK, TOK), F32)], axis=0
    )
    rope = rope.T.astype(BF16)
    for h in range(2):
        key = h * (NOPE + VDIM)
        value = key + NOPE
        for m in range(MICRO):
            for core in range(2):
                rows = slice(m * BLK + core * HALF, m * BLK + (core + 1) * HALF)
                for chip in range(2):
                    at = 8 * h + 4 * m + 2 * chip + core
                    out_ref[at, :, :VDIM] = expanded[rows, value : value + VDIM]
                    out_ref[at, :, VDIM : VDIM + NOPE] = expanded[rows, key : key + NOPE]
                    out_ref[at, :, VDIM + NOPE :] = rope[rows, :]


def expand(latent_t, cos_t, sin_t, gain, w_expand):
    return pl.pallas_call(
        expand_kernel,
        out_shape=(
            jax.ShapeDtypeStruct((KVL, TOK), BF16),
            jax.ShapeDtypeStruct((ROWS, HALF, PACK), BF16),
        ),
        compiler_params=pltpu.CompilerParams(vmem_limit_bytes=60 * MIB),
        cost_estimate=pl.CostEstimate(flops=TOK * D * 256, bytes_accessed=MIB, transcendentals=0),
    )(latent_t, cos_t, sin_t, gain.reshape(KVL, 1), w_expand)


def latent_back_kernel(
    pack_ref, latent_ref, cos_ref, sin_ref, gain_ref, w_ref, d_exp_ref, d_latent_ref, gg_ref
):
    rope = [None] * (2 * MICRO)
    for h in range(2):
        for m in range(MICRO):
            for core in range(2):
                at = 8 * h + 4 * m + core
                part = pack_ref[at].astype(F32) + pack_ref[at + 2].astype(F32)
                rows = slice(m * BLK + core * HALF, m * BLK + (core + 1) * HALF)
                key = h * (NOPE + VDIM)
                d_exp_ref[rows, key : key + NOPE] = part[:, VDIM : VDIM + NOPE].astype(BF16)
                d_exp_ref[rows, key + NOPE : key + NOPE + VDIM] = part[:, :VDIM].astype(BF16)
                piece = part[:, VDIM + NOPE :]
                at = 2 * m + core
                rope[at] = piece if h == 0 else rope[at] + piece
    rope = jnp.concatenate(rope, axis=0).T
    half = ROPE // 2
    a, b = rope[:half], rope[half:ROPE]
    cos, sin = cos_ref[...], sin_ref[...]
    d_latent_ref[KVL : KVL + half, :] = (a * cos + b * sin).astype(BF16)
    d_latent_ref[KVL + half :, :] = (b * cos - a * sin).astype(BF16)
    d_normed = matmul_nt(w_ref[...], d_exp_ref[...])
    c = latent_ref[:KVL, :].astype(F32)
    scale = lax.rsqrt(jnp.mean(c * c, axis=0, keepdims=True) + EPS)
    gg_ref[...] = jnp.sum(d_normed * c * scale, axis=1, keepdims=True)
    weighted = d_normed * gain_ref[...]
    inner = jnp.mean(weighted * c, axis=0, keepdims=True)
    d_latent_ref[:KVL, :] = (scale * weighted - c * (scale * scale * scale) * inner).astype(BF16)


def latent_back(pack, latent_t, cos_t, sin_t, gain, w_expand):
    return pl.pallas_call(
        latent_back_kernel,
        out_shape=(
            jax.ShapeDtypeStruct((TOK, 2 * (NOPE + VDIM)), BF16),
            jax.ShapeDtypeStruct((LAT, TOK), BF16),
            jax.ShapeDtypeStruct((KVL, 1), F32),
        ),
        compiler_params=pltpu.CompilerParams(vmem_limit_bytes=60 * MIB),
        cost_estimate=pl.CostEstimate(flops=TOK * D * 256, bytes_accessed=MIB, transcendentals=0),
    )(pack, latent_t, cos_t, sin_t, gain.reshape(KVL, 1), w_expand)


def hidden_kernel(mid_ref, grad_ref, gate_ref, spread_ref, wg_ref, wu_ref, wd_ref, out_ref):
    mid = mid_ref[...]
    pre = matmul(mid, wg_ref[...])
    up = matmul(mid, wu_ref[...])
    back = matmul(grad_ref[...], wd_ref[...])
    gate = matmul(gate_ref[...], spread_ref[...])
    sig = 1.0 / (1.0 + jnp.exp(-pre))
    act = pre * sig
    back = back * gate
    out_ref[0] = (back * up * (sig * (1.0 + pre * (1.0 - sig)))).astype(BF16)
    out_ref[1] = (back * act).astype(BF16)
    out_ref[2] = (act * up * gate).astype(BF16)


def hidden(mid, grad, gates, spread, weights):
    whole = pl.BlockSpec((TOK, D), lambda j: (0, 0))
    parts = HID // BLK

    def weight(at):
        return pl.BlockSpec((D, BLK), lambda j: (0, at * parts + j))

    return pl.pallas_call(
        hidden_kernel,
        grid=(parts,),
        out_shape=jax.ShapeDtypeStruct((3, TOK, HID), BF16),
        in_specs=[
            whole,
            whole,
            pl.BlockSpec(gates.shape, lambda j: (0, 0)),
            pl.BlockSpec((spread.shape[0], BLK), lambda j: (0, j)),
            weight(0),
            weight(1),
            weight(2),
        ],
        out_specs=pl.BlockSpec((3, TOK, BLK), lambda j: (0, 0, j)),
        compiler_params=pltpu.CompilerParams(vmem_limit_bytes=60 * MIB),
        cost_estimate=pl.CostEstimate(
            flops=2 * TOK * D * HID * 3, bytes_accessed=32 * MIB, transcendentals=TOK * HID
        ),
    )(mid, grad, gates, spread, weights, weights, weights)


def mid_grad_kernel(hid_ref, w_ref, out_ref):
    out = matmul_nt(hid_ref[0], w_ref[:, :HID]) + matmul_nt(hid_ref[1], w_ref[:, HID:])
    out_ref[...] = out.astype(BF16)


def mid_grad(hid, weights):
    return pl.pallas_call(
        mid_grad_kernel,
        grid=(COLS,),
        out_shape=jax.ShapeDtypeStruct((TOK, D), BF16),
        in_specs=[
            pl.BlockSpec((2, TOK, HID), lambda j: (0, 0, 0)),
            pl.BlockSpec((FEAT, 2 * HID), lambda j: (j, 0)),
        ],
        out_specs=pl.BlockSpec((TOK, FEAT), lambda j: (0, j)),
        compiler_params=pltpu.CompilerParams(vmem_limit_bytes=60 * MIB),
        cost_estimate=pl.CostEstimate(
            flops=2 * TOK * D * HID * 2, bytes_accessed=20 * MIB, transcendentals=0
        ),
    )(hid, weights)


def output_kernel(col_ref, hid_ref, w_ref, residual_ref, out_ref):
    out_ref[0] = matmul_nt(hid_ref[0], w_ref[...]).astype(BF16)
    own = pl.ds(pl.multiple_of(col_ref[0] * OWN, OWN), OWN)
    out_ref[0, own, :] = (
        matmul_nt(hid_ref[0, own, :], w_ref[...]) + residual_ref[...]
    ).astype(BF16)


def output(col, hid, weights, residual):
    return pl.pallas_call(
        output_kernel,
        grid=(COLS,),
        out_shape=jax.ShapeDtypeStruct((COLS, TOK, FEAT), BF16),
        in_specs=[
            pl.BlockSpec(memory_space=pltpu.SMEM),
            pl.BlockSpec((1, TOK, HID), lambda j: (2, 0, 0)),
            pl.BlockSpec((FEAT, HID), lambda j: (j, 2)),
            pl.BlockSpec((OWN, FEAT), lambda j: (0, j)),
        ],
        out_specs=pl.BlockSpec((1, TOK, FEAT), lambda j: (j, 0, 0)),
        compiler_params=pltpu.CompilerParams(vmem_limit_bytes=60 * MIB),
        cost_estimate=pl.CostEstimate(
            flops=TOK * D * HID // 8, bytes_accessed=MIB, transcendentals=0
        ),
    )(col.astype(jnp.int32).reshape(1), hid, weights, residual)


def mid_kernel(parts_ref, inputs_ref, gain_ref, residual_ref, scale_ref, normed_ref):
    total = inputs_ref[...].astype(F32)
    for c in range(COLS):
        total = total + parts_ref[c].astype(F32)
    scale = inverse_rms(total)
    residual_ref[...] = total
    scale_ref[...] = scale
    normed = (total * scale * gain_ref[...]).astype(BF16)
    for c in range(COLS):
        normed_ref[c] = normed


def mid(parts, inputs, gain):
    return pl.pallas_call(
        mid_kernel,
        out_shape=(
            jax.ShapeDtypeStruct((OWN, D), F32),
            jax.ShapeDtypeStruct((OWN, 1), F32),
            jax.ShapeDtypeStruct((COLS, OWN, D), BF16),
        ),
        compiler_params=pltpu.CompilerParams(vmem_limit_bytes=60 * MIB),
        cost_estimate=pl.CostEstimate(
            flops=OWN * D * 16, bytes_accessed=5 * MIB, transcendentals=0
        ),
    )(parts, inputs, gain.reshape(1, D))


def mid_back_kernel(
    parts_ref, residual_ref, scale_ref, grad_ref, gain_ref, out_ref, low_ref, gain_grad_ref
):
    d_mid = parts_ref[0].astype(F32)
    for c in range(1, COLS):
        d_mid = d_mid + parts_ref[c].astype(F32)
    residual, scale = residual_ref[...], scale_ref[...]
    gain_grad_ref[...] = jnp.sum(d_mid * residual * scale, axis=0, keepdims=True)
    out = grad_ref[...].astype(F32) + norm_backward(d_mid, residual, scale, gain_ref[...])
    out_ref[...] = out
    low = out.astype(BF16)
    for c in range(COLS):
        low_ref[c] = low


def mid_back(parts, residual, scale, grad, gain):
    return pl.pallas_call(
        mid_back_kernel,
        out_shape=(
            jax.ShapeDtypeStruct((OWN, D), F32),
            jax.ShapeDtypeStruct((COLS, OWN, D), BF16),
            jax.ShapeDtypeStruct((1, D), F32),
        ),
        compiler_params=pltpu.CompilerParams(vmem_limit_bytes=60 * MIB),
        cost_estimate=pl.CostEstimate(
            flops=OWN * D * 24, bytes_accessed=5 * MIB, transcendentals=0
        ),
    )(parts, residual, scale, grad, gain.reshape(1, D))


def input_back_kernel(
    col_ref, dq_ref, dl_ref, wq_ref, wl_ref, x_ref, scale_ref, gain_ref, own_ref, out_ref, gg_ref
):
    step = pl.program_id(0)
    first = col_ref[1]
    d_in = matmul_nt(dq_ref[...], wq_ref[...]) + matmul_nt(dl_ref[...], wl_ref[...])
    x, scale = x_ref[...].astype(F32), scale_ref[...]
    gain_grad = jnp.sum(d_in * x * scale, axis=0, keepdims=True)

    @pl.when(step == 0)
    def _():
        gg_ref[...] = gain_grad

    @pl.when(step > 0)
    def _():
        gg_ref[...] += gain_grad

    out = norm_backward(d_in, x, scale, gain_ref[...])
    for half in range(2):
        mine = (col_ref[0] == first + 2 * step + half).astype(F32)
        rows = slice(half * OWN, (half + 1) * OWN)
        part = (out[rows] + mine * own_ref[...]).astype(BF16)
        for c in range(COLS):
            out_ref[c, rows, :] = part[:, c * FEAT : (c + 1) * FEAT]


def input_back(col, tree, d_query, d_latent, w_query, w_latent, inputs, scale, gain, own):
    rows = 2 * OWN
    steps = BLK // rows
    widths = (d_query.shape[1], d_latent.shape[1])
    return pl.pallas_call(
        input_back_kernel,
        grid=(steps,),
        out_shape=(
            jax.ShapeDtypeStruct((COLS, BLK, FEAT), BF16),
            jax.ShapeDtypeStruct((1, D), F32),
        ),
        in_specs=[
            pl.BlockSpec(memory_space=pltpu.SMEM),
            pl.BlockSpec((rows, widths[0]), lambda j: (steps * tree + j, 0)),
            pl.BlockSpec((rows, widths[1]), lambda j: (steps * tree + j, 0)),
            pl.BlockSpec((D, widths[0]), lambda j: (0, 0)),
            pl.BlockSpec((D, widths[1]), lambda j: (0, 0)),
            pl.BlockSpec((rows, D), lambda j: (steps * tree + j, 0)),
            pl.BlockSpec((rows, 1), lambda j: (steps * tree + j, 0)),
            pl.BlockSpec((1, D), lambda j: (0, 0)),
            pl.BlockSpec((OWN, D), lambda j: (0, 0)),
        ],
        out_specs=(
            pl.BlockSpec((COLS, rows, FEAT), lambda j: (0, j, 0)),
            pl.BlockSpec((1, D), lambda j: (0, 0)),
        ),
        compiler_params=pltpu.CompilerParams(vmem_limit_bytes=60 * MIB),
        cost_estimate=pl.CostEstimate(
            flops=2 * TOK * D * 640, bytes_accessed=9 * MIB, transcendentals=0
        ),
    )(
        jnp.stack([col.astype(jnp.int32), jnp.int32(tree * BLK // OWN)]),
        d_query,
        d_latent,
        w_query,
        w_latent,
        inputs,
        scale,
        gain.reshape(1, D),
        own,
    )


def weight_grad(mid_ref, grad_ref, hid_ref):
    lhs = jnp.where(pl.program_id(0) == 2, grad_ref[...], mid_ref[...])
    return matmul(lhs, hid_ref[0])


def send_grad_kernel(mid_ref, grad_ref, hid_ref, out_ref):
    out_ref[...] = weight_grad(mid_ref, grad_ref, hid_ref).astype(BF16)


def keep_grad_kernel(mid_ref, grad_ref, hid_ref, got_ref, o0, o1, o2, o3):
    out = weight_grad(mid_ref, grad_ref, hid_ref) + got_ref[...].astype(F32)
    for j, ref in enumerate((o0, o1, o2, o3)):
        ref[...] = out[j * LANES : (j + 1) * LANES].astype(BF16)


def send_grads(mid_t, grad_t, hid):
    width = HID // 2
    rows = D // 2
    whole = pl.BlockSpec((rows, TOK), lambda s, j: (1, 0))
    return pl.pallas_call(
        send_grad_kernel,
        grid=(3, 2),
        out_shape=jax.ShapeDtypeStruct((rows, WIDE), BF16),
        in_specs=[whole, whole, pl.BlockSpec((1, TOK, width), lambda s, j: (s, 0, j))],
        out_specs=pl.BlockSpec((rows, width), lambda s, j: (0, 2 * s + j)),
        compiler_params=pltpu.CompilerParams(vmem_limit_bytes=60 * MIB),
        cost_estimate=pl.CostEstimate(
            flops=TOK * D * HID // 32, bytes_accessed=MIB, transcendentals=0
        ),
    )(mid_t, grad_t, hid)


def keep_grads(z, mid_t, grad_t, hid, got):
    width = HID // 2
    rows = D // 4
    whole = pl.BlockSpec((rows, TOK), lambda s, j: (z, 0))
    block = pl.BlockSpec((LANES, width), lambda s, j: (0, 2 * s + j))
    return pl.pallas_call(
        keep_grad_kernel,
        grid=(3, 2),
        out_shape=[jax.ShapeDtypeStruct((LANES, WIDE), BF16)] * 4,
        in_specs=[
            whole,
            whole,
            pl.BlockSpec((1, TOK, width), lambda s, j: (s, 0, j)),
            pl.BlockSpec((rows, width), lambda s, j: (z, 2 * s + j)),
        ],
        out_specs=[block] * 4,
        compiler_params=pltpu.CompilerParams(vmem_limit_bytes=60 * MIB),
        cost_estimate=pl.CostEstimate(
            flops=TOK * D * HID // 32, bytes_accessed=MIB, transcendentals=0
        ),
    )(mid_t, grad_t, hid, got)


def pack_hidden(shared, routed):
    rows = shared.shape[0]
    return jnp.concatenate(
        [
            shared,
            jnp.swapaxes(routed, 0, 1).reshape(rows, EXPERTS * ROUTED),
            jnp.zeros((rows, HID - SHARED - EXPERTS * ROUTED), routed.dtype),
        ],
        axis=1,
    )


def local(
    tokens,
    out_grad,
    parents,
    routes,
    gates,
    norm_in,
    w_query,
    w_latent,
    norm_latent,
    w_expand,
    w_output,
    norm_mid,
    w_shared_gate,
    w_shared_up,
    w_shared_down,
    w_expert_gate,
    w_expert_up,
    w_expert_down,
):
    row = lax.axis_index("row")
    col = lax.axis_index("col")
    group = row // QUART
    own_start = col * OWN
    gain_in = norm_in.astype(F32)
    gain_latent = norm_latent.astype(F32)
    gain_mid = norm_mid.astype(F32)
    heads = 2

    query_pack = w_query.reshape(D // ROWS, heads, QK)
    attn_pack = jnp.concatenate(
        [
            query_pack[:, :, :NOPE].reshape(D // ROWS, heads * NOPE),
            query_pack[:, :, NOPE:].reshape(D // ROWS, heads * ROPE),
            w_expand.reshape(KVL // ROWS, 4, 128).transpose(1, 0, 2).reshape(D // ROWS, 128),
            w_latent,
            jnp.zeros((D // ROWS, 128 - LATC), BF16),
            w_output.T,
        ],
        axis=1,
    )
    ffn_pack = jnp.concatenate(
        [
            pack_hidden(w_shared_gate, w_expert_gate),
            pack_hidden(w_shared_up, w_expert_up),
            pack_hidden(w_shared_down.T, jnp.swapaxes(w_expert_down, 1, 2)),
        ],
        axis=1,
    )
    attn_pair, input_pair, ffn_pack = together(
        pair_up(attn_pack, "row"), pair_up(tokens.reshape(TOK, FEAT), "col"), ffn_pack
    )
    attn_ring = ring_up(attn_pair, "row")
    input_ring = ring_up(input_pair, "col")
    ffn_other = trade(ffn_pack, "row", 8)
    ffn_pack, attn_ring, input_ring = together(ffn_pack, attn_ring, input_ring)
    ffn_near = near_shards(ffn_pack)
    attn_full = finish_rows(attn_ring, row)
    query_full = attn_full[:, : heads * QK]
    expand_full = attn_full[:, 384:512].reshape(ROWS, 4, KVL // ROWS, 128)
    expand_full = expand_full.transpose(0, 2, 1, 3).reshape(KVL, heads * (NOPE + VDIM))
    latent_full = attn_full[:, 512:640]
    output_full = attn_full[:, 640:]

    seg = jnp.maximum(row - (TRUNK // BLK - 1), 0).astype(jnp.int32)
    depths = ancestor_depths(parents, seg.reshape(1))
    starts = jnp.where(seg > 0, TRUNK + BLK * depths, BLK * row)
    positions = (starts[:, None] + jnp.arange(BLK, dtype=jnp.int32)[None, :]).reshape(TOK)
    frequency = THETA ** (-jnp.arange(ROPE // 2, dtype=F32) / (ROPE // 2))
    angles = positions.astype(F32)[:, None] * frequency[None, :]
    cos_table, sin_table = jnp.cos(angles), jnp.sin(angles)

    cos_t, sin_t = cos_table.T, sin_table.T
    cos_wide, sin_wide = jnp.tile(cos_table, (1, 4)), jnp.tile(sin_table, (1, 4))

    inputs, normed_in, scale_in, latent_parts = front(col, input_ring, gain_in, latent_full)
    query = project_query(group, normed_in, query_full, cos_wide, sin_wide)
    latent_t, query, normed_in, ffn_near, ffn_other = together(
        swap(latent_parts, "col"), trade_quarter(query), normed_in, ffn_near, ffn_other
    )
    latent_t = latent_t.reshape(LAT, TOK)
    latent_normed_t, pack = expand(latent_t, cos_t, sin_t, gain_latent, expand_full)
    near, ffn_near = together(swap(pack, "row"), ffn_near)
    ffn_far = far_halves(ffn_near)
    grad_blocks = share(after(out_grad, near).reshape(TOK, FEAT), "col", COLS)
    far = trade(near, "row", 1)

    meta = jnp.concatenate([pick(parents, group % MICRO), smem_values(row % QUART, group)])
    *attended_own, lse = attend(meta, query, near, far)
    attended_own, lse, ffn_far = together(attended_own, lse, ffn_far)
    attended_parts, grad_blocks, ffn_far, ffn_other = together(
        trade_quarter(attended_own), grad_blocks, ffn_far, ffn_other
    )
    attended, attn_parts = project(group, attended_parts, output_full)
    grad_full, grad_t = features(row, grad_blocks)

    def both_cores(pieces):
        far_pieces = [(trade(v, "row", 1), apart ^ 1, first) for v, apart, first in pieces]
        return list(pieces) + far_pieces

    pieces = both_cores(
        [(ffn_pack, 0, 0), (ffn_near[0], 2, 0), (ffn_near[1], 6, 0)]
        + [(ffn_far[0], 4, 0), (ffn_far[1], 4, CUT)]
    )
    own_inputs = lax.dynamic_slice_in_dim(inputs, own_start, OWN, 0)
    attn_parts, grad_full, grad_t, other_near, values = together(
        swap(attn_parts, "col"),
        grad_full,
        grad_t,
        near_shards(ffn_other),
        [v for v, _, _ in pieces],
    )
    residual, scale_mid, normed_mid = mid(attn_parts, own_inputs, gain_mid)
    pieces = [(v, apart, first) for v, (_, apart, first) in zip(values, pieces)]
    ffn_full = put_shards(row, None, pieces)
    pieces = both_cores([(ffn_other, 8, 0), (other_near[0], 10, 0), (other_near[1], 14, 0)])
    ffn_full = put_shards(row, ffn_full, pieces)
    normed_mid, ffn_full, other_far = together(
        swap(normed_mid, "col"), ffn_full, far_halves(other_near)
    )
    normed_mid = normed_mid.reshape(TOK, D)
    pieces = both_cores([(other_far[0], 12, 0), (other_far[1], 12, CUT)])
    ffn_full = put_shards(row, ffn_full, pieces)

    named = routes.reshape(TOK, TOPK, 1) == jnp.arange(EXPERTS, dtype=jnp.int32)
    gate_of = jnp.sum(jnp.where(named, gates.reshape(TOK, TOPK, 1), 0.0), axis=1)
    gate_of = jnp.concatenate(
        [jnp.ones((TOK, 1), F32), gate_of, jnp.zeros((TOK, 15 - EXPERTS), F32)], axis=1
    )
    gate_high = gate_of.astype(BF16)
    gate_low = (gate_of - gate_high.astype(F32)).astype(BF16)
    unit = jnp.arange(HID, dtype=jnp.int32)
    expert = jnp.where(unit < SHARED, 0, 1 + (unit - SHARED) // ROUTED)
    spread = (expert[None, :] == jnp.arange(16, dtype=jnp.int32)[:, None]).astype(BF16)
    hid = hidden(
        normed_mid,
        grad_full,
        jnp.concatenate([gate_high, gate_low], axis=1),
        jnp.concatenate([spread, spread], axis=0),
        ffn_full,
    )
    normed_t = turn(row, after(normed_mid, hid))
    send = send_grads(normed_t, grad_t, hid)
    hid, send, normed_t = together(hid, send, normed_t)
    mid_parts = mid_grad(hid, ffn_full)
    hid, normed_t, mid_parts = together(hid, normed_t, mid_parts)
    got = trade(send, "row", 1)
    blocks = keep_grads(1, normed_t, grad_t, hid, got)
    own_blocks = keep_grads(0, normed_t, grad_t, after(hid, blocks), got)
    mid_parts, hid, blocks, halves, own_blocks = together(
        swap(mid_parts.reshape(COLS, OWN, D), "col"), hid, blocks, sum_opposite(blocks), own_blocks
    )
    own_grad = lax.dynamic_slice_in_dim(grad_full, own_start, OWN, 0)
    d_residual, d_low, mid_gain = mid_back(mid_parts, residual, scale_mid, own_grad, gain_mid)
    d_low, hid, sides = together(d_low, hid, with_opposite(blocks, halves))
    d_low, out_parts, sides = together(
        swap(d_low, "col"), output(col, hid, ffn_full, residual), sum_neighbours(sides)
    )
    other_sum = add_low(blocks[0].astype(F32) + sides[0].astype(F32), sides[1])

    d_attended = trade_quarter(project_back(group, d_low, output_full))
    out_parts = collect_y(out_parts, col // 2)
    d_attended, other_sum = together(d_attended, other_sum)
    *d_query, d_near, d_far = attend_back(
        meta, query, attended_own, d_attended, near, far, lse
    )
    d_query, d_near, d_far, halves, other_low, out_parts = together(
        d_query,
        d_near,
        d_far,
        sum_opposite(own_blocks),
        trade(other_sum[:, :CUT], "row", 8),
        out_parts,
    )
    d_far = trade(d_far, "row", 1)
    d_query, d_pack, out_parts = together(
        trade_quarter(d_query), add_low(d_near, d_far), out_parts
    )
    layer_out = collect_z(out_parts, col % 2).astype(BF16)
    d_pack, layer_out, sides = together(
        swap(d_pack, "row"), layer_out, with_opposite(own_blocks, halves)
    )
    sides = sum_neighbours(sides)

    d_expanded, d_latent, latent_gain = latent_back(
        d_pack, latent_t, cos_t, sin_t, gain_latent, expand_full
    )
    d_query = query_back(group, d_query, cos_wide, sin_wide)
    d_latent, d_query = together(swap(d_latent.reshape(COLS, LATC, TOK), "col"), d_query)
    d_latent = jnp.sum(d_latent.astype(F32), axis=0).astype(BF16)
    d_latent = jnp.concatenate([d_latent, jnp.zeros((128 - LATC, TOK), BF16)], axis=0).T

    d_tokens = []
    for tree in range(MICRO):
        part, gain_part = input_back(
            col,
            tree,
            d_query,
            d_latent,
            query_full,
            latent_full,
            inputs,
            scale_in,
            gain_in,
            d_residual,
        )
        in_gain = gain_part if tree == 0 else in_gain + gain_part
        d_tokens.append(part)
    attn_grads = attn_weight_grads(
        row, normed_in, d_query, d_latent, d_low.reshape(TOK, D), attended, latent_normed_t, d_expanded
    )
    first, second, in_gain, attn_grads, sides = together(
        swap(d_tokens[0], "col"), d_tokens[1], in_gain, attn_grads, sides
    )
    attn_grads = reduce_row(*attn_grads)
    gain = jnp.concatenate([in_gain.reshape(D), latent_gain.reshape(KVL), mid_gain.reshape(D)])
    second = swap(second, "col")
    gain = share(after(gain.astype(BF16).reshape(-1, 128), second), ("row", "col"), ROWS * COLS)
    gain = jnp.sum(gain.astype(F32), axis=0).reshape(-1)
    other_high = trade(after(other_sum, second)[:, CUT:], "row", 8)
    grad_query = jnp.concatenate(
        [
            attn_grads[:, : heads * NOPE].reshape(-1, heads, NOPE),
            attn_grads[:, heads * NOPE : heads * QK].reshape(-1, heads, ROPE),
        ],
        axis=-1,
    ).reshape(-1, heads * QK)
    grad_output = attn_grads[:, 384:640].T
    grad_expand = attn_grads[:, 640:768].reshape(4, KVL // ROWS, 128)
    grad_expand = grad_expand.transpose(1, 0, 2).reshape(KVL // ROWS, heads * (NOPE + VDIM))
    grad_latent = attn_grads[:, 768 : 768 + LATC]

    ffn_grads = own_blocks[0].astype(F32) + sides[0].astype(F32) + sides[1].astype(F32)
    other_sum = jnp.concatenate([other_low, other_high], axis=1)
    ffn_grads = ffn_grads + other_sum.astype(F32)

    def unpack(at):
        part = ffn_grads[:, at * HID : (at + 1) * HID]
        routed = part[:, SHARED : SHARED + EXPERTS * ROUTED]
        return part[:, :SHARED], routed.reshape(-1, EXPERTS, ROUTED)

    grad_shared_gate, grad_expert_gate = unpack(0)
    grad_shared_up, grad_expert_up = unpack(1)
    grad_shared_down, grad_expert_down = unpack(2)
    ffn_outs = (
        grad_shared_gate,
        grad_shared_up,
        grad_shared_down.T,
        jnp.swapaxes(grad_expert_gate, 0, 1),
        jnp.swapaxes(grad_expert_up, 0, 1),
        grad_expert_down.transpose(1, 2, 0),
    )
    input_grad = jnp.stack([first, second])
    input_grad = jnp.sum(input_grad.astype(F32), axis=1).astype(BF16)
    return (
        layer_out.reshape(MICRO, BLK, FEAT),
        input_grad,
        gain[:D],
        grad_query,
        grad_latent,
        gain[D : D + KVL],
        grad_expand,
        grad_output,
        gain[D + KVL :],
        *ffn_outs,
    )


def solution(mesh):
    in_specs = (
        P(None, "row", "col"),
        P(None, "row", "col"),
        P(),
        P(None, "row", None),
        P(None, "row", None),
        P(),
        P("row", "col"),
        P("row", "col"),
        P(),
        P("row", "col"),
        P("col", "row"),
        P(),
        P("row", "col"),
        P("row", "col"),
        P("col", "row"),
        P(None, "row", "col"),
        P(None, "row", "col"),
        P(None, "col", "row"),
    )
    out_specs = (
        P(None, "row", "col"),
        P(None, "row", "col"),
        P(),
        P("row", "col"),
        P("row", "col"),
        P(),
        P("row", "col"),
        P("col", "row"),
        P(),
        P("row", "col"),
        P("row", "col"),
        P("col", "row"),
        P(None, "row", "col"),
        P(None, "row", "col"),
        P(None, "col", "row"),
    )
    return jax.shard_map(local, mesh=mesh, in_specs=in_specs, out_specs=out_specs, check_vma=False)
```

time: 783 us -> 634 us (0.81)
  waiting for transfers between devices: 337 us -> 165 us
  Pallas kernels: 78.5 us -> 191 us
  starting transfers between devices: 84.4 us -> 130 us
  local copies, waits for them, and re-layouts: 106 us -> 60.5 us
  matrix products: 27.3 us -> 0 us
  other arithmetic: 50.2 us -> 25.7 us
  blocking collectives: 71.5 us -> 48.4 us
  between operations: 15.5 us -> 1.85 us
    all_to_all x16 -> x10, waiting for transfers between devices: 309 us -> 19 us  [swap(): lax.all_to_all(values, axis, 0, 0, tiled=True, axis_index_groups=groups)]
    ppermute x0 -> x62, waiting for transfers between devices: none -> 146 us  [trade(): return lax.ppermute(values, axis, [(i, i ^ mask) for i in range(count)])]
    pallas_call x4 -> x27, Pallas kernels: 59.8 us -> 171 us  [the longest x2 19.3 us: keep_grads(): pl.pallas_call(keep_grad_kernel, grid=(3, 2), out_shape=[jax.ShapeDtypeSt...]
    ppermute x0 -> x62, starting transfers between devices: none -> 83.8 us  [trade(): return lax.ppermute(values, axis, [(i, i ^ mask) for i in range(count)])]
    all_to_all x16 -> x10, starting transfers between devices: 84.3 us -> 45.9 us  [swap(): lax.all_to_all(values, axis, 0, 0, tiled=True, axis_index_groups=groups)]
    all_gather x2 -> x0, waiting for transfers between devices: 27.3 us -> none  [the longest x1 27.3 us: local(): attn_full = lax.all_gather(attn_pack, 'row', axis=0, tiled=True)]
    dot_general x12 -> x0, matrix products: 27.3 us -> none  [the longest x4 15.2 us: matmul_nt(): return lax.dot_general(a, b, NT, preferred_element_type=F32)]
    all_to_all x3 -> x2, blocking collectives: 71.5 us -> 48.4 us  [swap(): lax.all_to_all(values, axis, 0, 0, tiled=True, axis_index_groups=groups)]
  transfers between devices with their start and end apart: 19 -> 72, of which waited for: 16 -> 32; matrix products, arithmetic and copies ran while one was open for 20% -> 11% of each run, Pallas kernels for 5% -> 22%
where the time goes in v2:
time: 634 us; the launch traced here: 623 us
  Pallas kernels  191 us (30%)
  waiting for transfers between devices  165 us (26%)
  starting transfers between devices  130 us (21%)
  local copies, waits for them, and re-layouts  60.5 us (10%)
  blocking collectives  48.4 us (8%)
  other arithmetic  25.7 us (4%)
    ppermute x62, waiting for transfers between devices, trade(): return lax.ppermute(values, axis, [(i, i ^ mask) for i in range(count)])  146 us
    ppermute x62, starting transfers between devices, trade(): return lax.ppermute(values, axis, [(i, i ^ mask) for i in range(count)])  83.8 us
    all_to_all x2, blocking collectives, swap(): lax.all_to_all(values, axis, 0, 0, tiled=True, axis_index_groups=groups)  48.4 us
    all_to_all x10, starting transfers between devices, swap(): lax.all_to_all(values, axis, 0, 0, tiled=True, axis_index_groups=groups)  45.9 us
    pallas_call x2, Pallas kernels, keep_grads(): pl.pallas_call(keep_grad_kernel, grid=(3, 2), out_shape=[jax.ShapeDtypeSt...  19.3 us
    pallas_call x1, Pallas kernels, hidden(): pl.pallas_call(hidden_kernel, grid=(parts,), out_shape=jax.ShapeDtypeStru...  19 us
    all_to_all x10, waiting for transfers between devices, swap(): lax.all_to_all(values, axis, 0, 0, tiled=True, axis_index_groups=groups)  19 us
    pallas_call x3, Pallas kernels, put_shards(): pl.pallas_call(functools.partial(put_kernel, places), out_shape=jax.Shape...  18.2 us
  transfers between devices with their start and end apart: 72, of which 32 were waited for; matrix products, arithmetic and copies ran while one was open for 11% of the time, Pallas kernels for 22%

profile of v2, /device:TPU:0, one launch (start us, length us, event | category | flops | bytes accessed | tf_op | source)
XLA Modules:
  0.0 622.7 jit_solution(10289843058815080877)
XLA Ops:
  37.4 7.3 %collective-permute-done.3 = bf16[2,128,896]{2,1,0:T(8,128)(2,1)S(1)} collective-permute-done((bf16[2,128,896]{2,1,0:T(8,128)(2,1)S(1)}, bf16[2,128,896]{2,1,0:T(8,128)(2,1)S(1)}, u32[]{:S(2)}, u32[]{:S(2)}) %collective-permute-start.3) | collective-permute-done | bytes 458784 | tf_op jit(solution)/shard_map/ppermute | solution.py:82
  44.7 8.5 %collective-permute-done.4 = bf16[2,128,896]{2,1,0:T(8,128)(2,1)S(1)} collective-permute-done((bf16[2,128,896]{2,1,0:T(8,128)(2,1)S(1)}, bf16[2,128,896]{2,1,0:T(8,128)(2,1)S(1)}, u32[]{:S(2)}, u32[]{:S(2)}) %collective-permute-start.4) | collective-permute-done | bytes 458784 | tf_op jit(solution)/shard_map/ppermute | solution.py:82
  105.0 28.1 %all_to_all.60.near_ref.refs_12_ = bf16[16,128,384]{2,1,0:T(8,128)(2,1)} all-to-all(bf16[16,128,384]{2,1,0:T(8,128)(2,1)} %get-tuple-element.222), channel_id=1, replica_groups=mesh['row'=16,'col'=8] {'row'}, dimensions={0} | all-to-all | bytes 3145728 | tf_op jit(solution)/shard_map/all_to_all | solution.py:73
  145.9 10.0 %shard_map.294 = (bf16[256,128]{1,0:T(8,128)(2,1)}, bf16[256,128]{1,0:T(8,128)(2,1)}, bf16[256,128]{1,0:T(8,128)(2,1)}, bf16[256,128]{1,0:T(8,128)(2,1)}, f32[4,1,256]{2,1,0:T(1,128)}) custom-call(s32[15]{0:T(128)} %pad_add_fusion.meta, bf16[256,256]{1,0:T(8,128)(2,1)} %get-tuple-element.217.q0.refs_0_, bf16[256,256]{1,0:T(8,128)(2,1)} %copy-done.49, ...), custom_call_target="tpu_custom_call" | custom-call | flops 1342177280 | bytes 4194304 | tf_op jit(solution)/shard_map/pallas_call | solution.py:410
  193.5 22.6 %collective-permute-done.21.refs_1_ = bf16[128,5376]{1,0:T(8,128)(2,1)S(1)} collective-permute-done((bf16[128,5376]{1,0:T(8,128)(2,1)}, bf16[128,5376]{1,0:T(8,128)(2,1)S(1)}, u32[]{:S(2)}, u32[]{:S(2)}) %collective-permute-start.21) | collective-permute-done | bytes 1376288 | tf_op jit(solution)/shard_map/ppermute | solution.py:82
  221.8 5.7 all-to-all-start.4
  233.4 8.3 %shard_map.298.refs_6_ = bf16[2048,5376]{1,0:T(8,128)(2,1)} custom-call(s32[1]{0:T(128)} %bitcast.23.own_ref, bf16[128,5376]{1,0:T(8,128)(2,1)} %copy-done.10, bf16[128,5376]{1,0:T(8,128)(2,1)} %collective-permute-done.12.refs_1_, bf16[128,5376]{1,0:T(8,128)(2,1)} %collective-permute-done.13.refs_2_, bf16[128,2688]{1,0:T(8,128)(2,1)} %collective-permute-done.16.refs_3_, ...), custom_call_target="tpu_custom_call" | custom-call | bytes 1048576 | tf_op jit(solution)/shard_map/pallas_call | solution.py:205
  241.7 6.6 %shard_map.299.refs_4_ = bf16[2048,5376]{1,0:T(8,128)(2,1)} custom-call(s32[1]{0:T(128)} %bitcast.23.own_ref, bf16[128,5376]{1,0:T(8,128)(2,1)} %collective-permute-done.14.refs_0_, bf16[128,5376]{1,0:T(8,128)(2,1)} %copy-done.13, bf16[128,5376]{1,0:T(8,128)(2,1)} %collective-permute-done.22.refs_2_, ...), custom_call_target="tpu_custom_call", output_to_operand_aliasing={{}: (7, {})} | custom-call | bytes 1048576 | tf_op jit(solution)/shard_map/pallas_call | solution.py:205
  250.3 7.5 %all-to-all-done.4 = bf16[8,64,2048]{2,1,0:T(8,128)(2,1)S(1)} async-done(((bf16[8,64,2048]{2,1,0:T(8,128)(2,1)}), bf16[8,64,2048]{2,1,0:T(8,128)(2,1)S(1)}, u32[]{:S(2)}, u32[]{:S(2)}) %all-to-all-start.4) | async-done | bytes 2097184 | tf_op jit(solution)/shard_map/all_to_all | solution.py:73
  264.7 19.0 %shard_map.301.hid_ref = bf16[3,512,1792]{2,1,0:T(8,128)(2,1)} custom-call(bf16[512,2048]{1,0:T(8,128)(2,1)} %bitcast.131, bf16[512,2048]{1,0:T(8,128)(2,1)} %get-tuple-element.268.grad_ref, bf16[512,32]{1,0:T(8,128)(2,1)} %copy.207.gate_ref, bf16[32,1792]{1,0:T(8,128)(2,1)} %add_convert_fusion.5.spread_ref, ...), custom_call_target="tpu_custom_call" | custom-call | flops 11274289152 | bytes 33554432 | tf_op jit(solution)/shard_map/pallas_call | solution.py:774
  287.1 12.0 %shard_map.303 = bf16[1024,5376]{1,0:T(8,128)(2,1)} custom-call(bf16[2048,512]{1,0:T(8,128)(2,1)} %shard_map.302.mid_ref, bf16[2048,512]{1,0:T(8,128)(2,1)} %get-tuple-element.273.grad_ref, bf16[3,512,1792]{2,1,0:T(8,128)(2,1)} %shard_map.301.hid_ref), custom_call_target="tpu_custom_call" | custom-call | flops 58720256 | bytes 1048576 | tf_op jit(solution)/shard_map/pallas_call | solution.py:989
  299.3 14.1 %shard_map.304 = bf16[512,2048]{1,0:T(8,128)(2,1)} custom-call(bf16[3,512,1792]{2,1,0:T(8,128)(2,1)} %shard_map.301.hid_ref, bf16[2048,5376]{1,0:T(8,128)(2,1)} %shard_map.300.wg_ref.wu_ref.wd_ref.w_ref), custom_call_target="tpu_custom_call" | custom-call | flops 7516192768 | bytes 20971520 | tf_op jit(solution)/shard_map/pallas_call | solution.py:801
  317.1 9.6 %shard_map.305 = (bf16[128,5376]{1,0:T(8,128)(2,1)}, bf16[128,5376]{1,0:T(8,128)(2,1)}, bf16[128,5376]{1,0:T(8,128)(2,1)}, bf16[128,5376]{1,0:T(8,128)(2,1)}) custom-call(bf16[2048,512]{1,0:T(8,128)(2,1)} %shard_map.302.mid_ref, bf16[2048,512]{1,0:T(8,128)(2,1)} %get-tuple-element.273.grad_ref, bf16[3,512,1792]{2,1,0:T(8,128)(2,1)} %shard_map.301.hid_ref, ...), custom_call_target="tpu_custom_call" | custom-call | flops 58720256 | bytes 1048576 | tf_op jit(solution)/shard_map/pallas_call | solution.py:1007
  331.9 9.7 %shard_map.306 = (bf16[128,5376]{1,0:T(8,128)(2,1)}, bf16[128,5376]{1,0:T(8,128)(2,1)}, bf16[128,5376]{1,0:T(8,128)(2,1)}, bf16[128,5376]{1,0:T(8,128)(2,1)}) custom-call(bf16[2048,512]{1,0:T(8,128)(2,1)} %shard_map.302.mid_ref, bf16[2048,512]{1,0:T(8,128)(2,1)} %get-tuple-element.273.grad_ref, bf16[3,512,1792]{2,1,0:T(8,128)(2,1)} %shard_map.301.hid_ref, ...), custom_call_target="tpu_custom_call" | custom-call | flops 58720256 | bytes 1048576 | tf_op jit(solution)/shard_map/pallas_call | solution.py:1007
  341.6 7.7 %all-to-all-done.5.parts_ref = bf16[8,64,2048]{2,1,0:T(8,128)(2,1)S(1)} async-done(((bf16[8,64,2048]{2,1,0:T(8,128)(2,1)}), bf16[8,64,2048]{2,1,0:T(8,128)(2,1)S(1)}, u32[]{:S(2)}, u32[]{:S(2)}) %all-to-all-start.5) | async-done | bytes 2097184 | tf_op jit(solution)/shard_map/all_to_all | solution.py:73
  368.6 11.1 %shard_map.309 = bf16[8,512,256]{2,1,0:T(8,128)(2,1)} custom-call(s32[1]{0:T(128)} %bitcast.3.col_ref, bf16[3,512,1792]{2,1,0:T(8,128)(2,1)} %shard_map.301.hid_ref, bf16[2048,5376]{1,0:T(8,128)(2,1)} %shard_map.300.wg_ref.wu_ref.wd_ref.w_ref, f32[64,2048]{1,0:T(8,128)} %get-tuple-element.290.residual_ref), custom_call_target="tpu_custom_call" | custom-call | flops 234881024 | bytes 1048576 | tf_op jit(solution)/shard_map/pallas_call | solution.py:826
  379.7 15.1 %collective-permute-done.38 = bf16[128,5376]{1,0:T(8,128)(2,1)S(1)} collective-permute-done((bf16[128,5376]{1,0:T(8,128)(2,1)}, bf16[128,5376]{1,0:T(8,128)(2,1)S(1)}, u32[]{:S(2)}, u32[]{:S(2)}) %collective-permute-start.38) | collective-permute-done | bytes 1376288 | tf_op jit(solution)/shard_map/ppermute | solution.py:82
  422.5 12.4 %shard_map.311 = (bf16[256,256]{1,0:T(8,128)(2,1)}, bf16[256,256]{1,0:T(8,128)(2,1)}, bf16[256,256]{1,0:T(8,128)(2,1)}, bf16[256,256]{1,0:T(8,128)(2,1)}, bf16[1...) custom-call(s32[15]{0:T(128)} %pad_add_fusion.meta, bf16[256,256]{1,0:T(8,128)(2,1)} %get-tuple-element.217.q0.refs_0_, ...), custom_call_target="tpu_custom_call" | custom-call | flops 3489660928 | bytes 10485760 | tf_op jit(solution)/shard_map/pallas_call | solution.py:484
  434.8 7.8 %collective-permute-done.47 = bf16[2,512,256]{2,1,0:T(8,128)(2,1)S(1)} collective-permute-done((bf16[2,512,256]{2,1,0:T(8,128)(2,1)}, bf16[2,512,256]{2,1,0:T(8,128)(2,1)S(1)}, u32[]{:S(2)}, u32[]{:S(2)}) %collective-permute-start.47) | collective-permute-done | bytes 524320 | tf_op jit(solution)/shard_map/ppermute | solution.py:82
  470.6 17.5 %collective-permute-done.53 = bf16[512,256]{1,0:T(8,128)(2,1)} collective-permute-done((bf16[512,256]{1,0:T(8,128)(2,1)}, bf16[512,256]{1,0:T(8,128)(2,1)}, u32[]{:S(2)}, u32[]{:S(2)}) %collective-permute-start.53) | collective-permute-done | bytes 262176 | tf_op jit(solution)/shard_map/ppermute | solution.py:82
  524.6 9.6 %shard_map.317 = (bf16[8,128,896]{2,1,0:T(8,128)(2,1)}, bf16[8,128,896]{2,1,0:T(8,128)(2,1)}) custom-call(s32[1]{0:T(128)} %bitcast.23.own_ref, bf16[512,2048]{1,0:T(8,128)(2,1)} %get-tuple-element.362.normed_ref.x_ref, bf16[512,384]{1,0:T(8,128)(2,1)} %shard_map.314.dq_ref, bf16[512,128]{1,0:T(8,128)(2,1)} %pad_bitcast_fusion.dl_ref, ...), custom_call_target="tpu_custom_call" | custom-call | flops 67108864 | bytes 1048576 | tf_op jit(solution)/shard_map/pallas_call | solution.py:282
  534.2 20.3 %all_to_all.61 = bf16[8,256,256]{2,1,0:T(8,128)(2,1)} all-to-all(bf16[8,256,256]{2,1,0:T(8,128)(2,1)} %get-tuple-element.371), channel_id=1, replica_groups=mesh['row'=16,'col'=8] {'col'}, dimensions={0} | all-to-all | bytes 2097152 | tf_op jit(solution)/shard_map/all_to_all | solution.py:73
  560.3 6.5 %all-to-all-start.11 = ((bf16[128,36,128]{2,1,0:T(8,128)(2,1)}), bf16[128,36,128]{2,1,0:T(8,128)(2,1)}, u32[]{:S(2)}, u32[]{:S(2)}) async-start(bf16[128,36,128]{2,1,0:T(8,128)(2,1)} %broadcast_in_dim.62), calls=%async_computation.11 | async-start | bytes 2621440 | tf_op jit(solution)/shard_map/all_to_all | solution.py:73
  568.1 16.8 %collective-permute-done.61 = bf16[128,2688]{1,0:T(8,128)(2,1)S(1)} collective-permute-done((bf16[128,2688]{1,0:T(8,128)(2,1)}, bf16[128,2688]{1,0:T(8,128)(2,1)S(1)}, u32[]{:S(2)}, u32[]{:S(2)}) %collective-permute-start.61) | collective-permute-done | bytes 688160 | tf_op jit(solution)/shard_map/ppermute | solution.py:82
  (371 shorter events, 327.2 us)
Async XLA Ops:
  22.7 30.5 %collective-permute-start.5 = (bf16[2,512,256]{2,1,0:T(8,128)(2,1)S(1)}, bf16[2,512,256]{2,1,0:T(8,128)(2,1)S(1)}, u32[]{:S(2)}, u32[]{:S(2)}) collective-permute-start(bf16[2,512,256]{2,1,0:T(8,128)(2,1)S(1)} %pad_maximum_fusion.1.p0), channel_id=1, source_target_pairs={{0,2},{1,3},{2,0},{3,1},{4,6},{5,7},{6,4},{7,5},{8,10},{9,11},{10,... | collective-permute-start | bytes 1572872 | tf_op jit(solution)/shard_map/ppermute | solution.py:82
  54.8 39.4 %collective-permute-start.14 = (bf16[128,5376]{1,0:T(8,128)(2,1)S(1)}, bf16[128,5376]{1,0:T(8,128)(2,1)}, u32[]{:S(2)}, u32[]{:S(2)}) collective-permute-start(bf16[128,5376]{1,0:T(8,128)(2,1)S(1)} %concatenate.35.refs_0_), channel_id=1, source_target_pairs={{0,64},{8,72},{16,80},{24,88},{32,96},{40,104},{48,112},{56,120},{... | collective-permute-start | bytes 4128776 | tf_op jit(solution)/shard_map/ppermute | solution.py:82
  57.4 40.2 %collective-permute-start.12 = (bf16[128,5376]{1,0:T(8,128)(2,1)S(1)}, bf16[128,5376]{1,0:T(8,128)(2,1)}, u32[]{:S(2)}, u32[]{:S(2)}) collective-permute-start(bf16[128,5376]{1,0:T(8,128)(2,1)S(1)} %concatenate.35.refs_0_), channel_id=1, source_target_pairs={{0,16},{8,24},{16,0},{24,8},{32,48},{40,56},{48,32},{56,40},{64,80... | collective-permute-start | bytes 4128776 | tf_op jit(solution)/shard_map/ppermute | solution.py:82
  57.8 39.9 %collective-permute-start.13 = (bf16[128,5376]{1,0:T(8,128)(2,1)S(1)}, bf16[128,5376]{1,0:T(8,128)(2,1)}, u32[]{:S(2)}, u32[]{:S(2)}) collective-permute-start(bf16[128,5376]{1,0:T(8,128)(2,1)S(1)} %concatenate.35.refs_0_), channel_id=1, source_target_pairs={{0,48},{8,56},{16,32},{24,40},{32,16},{40,24},{48,0},{56,8},{64,11... | collective-permute-start | bytes 4128776 | tf_op jit(solution)/shard_map/ppermute | solution.py:82
  70.6 30.3 %all-to-all-start = ((bf16[8,72,512]{2,1,0:T(8,128)(2,1)}), bf16[8,72,512]{2,1,0:T(8,128)(2,1)S(1)}, u32[]{:S(2)}, u32[]{:S(2)}) async-start(bf16[8,72,512]{2,1,0:T(8,128)(2,1)} %get-tuple-element.210), calls=%async_computation | async-start | bytes 1179648 | tf_op jit(solution)/shard_map/all_to_all | solution.py:73
  134.6 39.1 %all-to-all-start.2 = ((bf16[8,512,256]{2,1,0:T(8,128)(2,1)}), bf16[8,512,256]{2,1,0:T(8,128)(2,1)S(1)}, u32[]{:S(2)}, u32[]{:S(2)}) async-start(bf16[8,512,256]{2,1,0:T(8,128)(2,1)} %broadcast_in_dim.55), calls=%async_computation.2 | async-start | bytes 4194304 | tf_op jit(solution)/shard_map/all_to_all | solution.py:73
  145.4 41.0 %collective-permute-start.23 = (bf16[128,5376]{1,0:T(8,128)(2,1)S(1)}, bf16[128,5376]{1,0:T(8,128)(2,1)}, u32[]{:S(2)}, u32[]{:S(2)}) collective-permute-start(bf16[128,5376]{1,0:T(8,128)(2,1)S(1)} %concatenate.35.refs_0_), channel_id=1, source_target_pairs={{0,8},{8,0},{16,24},{24,16},{32,40},{40,32},{48,56},{56,48},{64,72... | collective-permute-start | bytes 4128776 | tf_op jit(solution)/shard_map/ppermute | solution.py:82
  145.4 41.0 %collective-permute-start.24 = (bf16[128,5376]{1,0:T(8,128)(2,1)}, bf16[128,5376]{1,0:T(8,128)(2,1)}, u32[]{:S(2)}, u32[]{:S(2)}) collective-permute-start(bf16[128,5376]{1,0:T(8,128)(2,1)} %collective-permute-done.12.refs_1_), channel_id=1, source_target_pairs={{0,8},{8,0},{16,24},{24,16},{32,40},{40,32},{48,56},{56,48},{64,72... | collective-permute-start | bytes 4128776 | tf_op jit(solution)/shard_map/ppermute | solution.py:82
  177.9 40.3 %all-to-all-start.3 = ((bf16[8,64,2048]{2,1,0:T(8,128)(2,1)}), bf16[8,64,2048]{2,1,0:T(8,128)(2,1)}, u32[]{:S(2)}, u32[]{:S(2)}) async-start(bf16[8,64,2048]{2,1,0:T(8,128)(2,1)} %get-tuple-element.245), calls=%async_computation.3 | async-start | bytes 4194304 | tf_op jit(solution)/shard_map/all_to_all | solution.py:73
  183.3 32.8 %collective-permute-start.21 = (bf16[128,5376]{1,0:T(8,128)(2,1)}, bf16[128,5376]{1,0:T(8,128)(2,1)S(1)}, u32[]{:S(2)}, u32[]{:S(2)}) collective-permute-start(bf16[128,5376]{1,0:T(8,128)(2,1)} %collective-permute-done.14.refs_0_), channel_id=1, source_target_pairs={{0,16},{8,24},{16,0},{24,8},{32,48},{40,56},{48,32},{56,40},{64,80... | collective-permute-start | bytes 4128776 | tf_op jit(solution)/shard_map/ppermute | solution.py:82
  184.5 33.8 %collective-permute-start.22 = (bf16[128,5376]{1,0:T(8,128)(2,1)}, bf16[128,5376]{1,0:T(8,128)(2,1)}, u32[]{:S(2)}, u32[]{:S(2)}) collective-permute-start(bf16[128,5376]{1,0:T(8,128)(2,1)} %collective-permute-done.14.refs_0_), channel_id=1, source_target_pairs={{0,48},{8,56},{16,32},{24,40},{32,16},{40,24},{48,0},{56,8},{64,11... | collective-permute-start | bytes 4128776 | tf_op jit(solution)/shard_map/ppermute | solution.py:82
  221.8 36.1 %all-to-all-start.4 = ((bf16[8,64,2048]{2,1,0:T(8,128)(2,1)}), bf16[8,64,2048]{2,1,0:T(8,128)(2,1)S(1)}, u32[]{:S(2)}, u32[]{:S(2)}) async-start(bf16[8,64,2048]{2,1,0:T(8,128)(2,1)} %get-tuple-element.254), calls=%async_computation.4 | async-start | bytes 4194304 | tf_op jit(solution)/shard_map/all_to_all | solution.py:73
  313.4 35.8 %all-to-all-start.5 = ((bf16[8,64,2048]{2,1,0:T(8,128)(2,1)}), bf16[8,64,2048]{2,1,0:T(8,128)(2,1)S(1)}, u32[]{:S(2)}, u32[]{:S(2)}) async-start(bf16[8,64,2048]{2,1,0:T(8,128)(2,1)} %bitcast.133), calls=%async_computation.5 | async-start | bytes 4194304 | tf_op jit(solution)/shard_map/all_to_all | solution.py:73
  357.8 38.4 %all-to-all-start.6 = ((bf16[8,64,2048]{2,1,0:T(8,128)(2,1)}), bf16[8,64,2048]{2,1,0:T(8,128)(2,1)S(1)}, u32[]{:S(2)}, u32[]{:S(2)}) async-start(bf16[8,64,2048]{2,1,0:T(8,128)(2,1)} %get-tuple-element.300), calls=%async_computation.6 | async-start | bytes 4194304 | tf_op jit(solution)/shard_map/all_to_all | solution.py:73
  361.4 33.4 %collective-permute-start.38 = (bf16[128,5376]{1,0:T(8,128)(2,1)}, bf16[128,5376]{1,0:T(8,128)(2,1)S(1)}, u32[]{:S(2)}, u32[]{:S(2)}) collective-permute-start(bf16[128,5376]{1,0:T(8,128)(2,1)} %get-tuple-element.302), channel_id=1, source_target_pairs={{0,16},{8,24},{16,0},{24,8},{32,48},{40,56},{48,32},{56,40},{64,80... | collective-permute-start | bytes 4128776 | tf_op jit(solution)/shard_map/ppermute | solution.py:82
  361.5 34.7 %collective-permute-start.39 = (bf16[128,5376]{1,0:T(8,128)(2,1)}, bf16[128,5376]{1,0:T(8,128)(2,1)}, u32[]{:S(2)}, u32[]{:S(2)}) collective-permute-start(bf16[128,5376]{1,0:T(8,128)(2,1)} %get-tuple-element.303), channel_id=1, source_target_pairs={{0,48},{8,56},{16,32},{24,40},{32,16},{40,24},{48,0},{56,8},{64,11... | collective-permute-start | bytes 4128776 | tf_op jit(solution)/shard_map/ppermute | solution.py:82
  366.0 56.3 %collective-permute-start.43 = (bf16[128,2688]{1,0:T(8,128)(2,1)}, bf16[128,2688]{1,0:T(8,128)(2,1)}, u32[]{:S(2)}, u32[]{:S(2)}) collective-permute-start(bf16[128,2688]{1,0:T(8,128)(2,1)} %get-tuple-element.489), channel_id=1, source_target_pairs={{0,16},{8,24},{16,0},{24,8},{32,48},{40,56},{48,32},{56,40},{64,80... | collective-permute-start | bytes 2064392 | tf_op jit(solution)/shard_map/ppermute | solution.py:82
  367.3 67.5 %collective-permute-start.44 = (bf16[128,2688]{1,0:T(8,128)(2,1)}, bf16[128,2688]{1,0:T(8,128)(2,1)}, u32[]{:S(2)}, u32[]{:S(2)}) collective-permute-start(bf16[128,2688]{1,0:T(8,128)(2,1)} %get-tuple-element.488), channel_id=1, source_target_pairs={{0,48},{8,56},{16,32},{24,40},{32,16},{40,24},{48,0},{56,8},{64,11... | collective-permute-start | bytes 2064392 | tf_op jit(solution)/shard_map/ppermute | solution.py:82
  416.2 29.1 %collective-permute-start.45 = (bf16[128,2688]{1,0:T(8,128)(2,1)S(1)}, bf16[128,2688]{1,0:T(8,128)(2,1)S(1)}, u32[]{:S(2)}, u32[]{:S(2)}) collective-permute-start(bf16[128,2688]{1,0:T(8,128)(2,1)S(1)} %slice.144), channel_id=1, source_target_pairs={{0,64},{8,72},{16,80},{24,88},{32,96},{40,104},{48,112},{56,120},{... | collective-permute-start | bytes 2064392 | tf_op jit(solution)/shard_map/ppermute | solution.py:82
  458.5 31.3 %all-to-all-start.7 = ((bf16[16,128,384]{2,1,0:T(8,128)(2,1)}), bf16[16,128,384]{2,1,0:T(8,128)(2,1)S(1)}, u32[]{:S(2)}, u32[]{:S(2)}) async-start(bf16[16,128,384]{2,1,0:T(8,128)(2,1)} %add_convert_fusion.1), calls=%async_computation.7 | async-start | bytes 3145728 | tf_op jit(solution)/shard_map/all_to_all | solution.py:73
  498.2 36.0 %collective-permute-start.54 = (bf16[128,5376]{1,0:T(8,128)(2,1)}, bf16[128,5376]{1,0:T(8,128)(2,1)}, u32[]{:S(2)}, u32[]{:S(2)}) collective-permute-start(bf16[128,5376]{1,0:T(8,128)(2,1)} %get-tuple-element.368), channel_id=1, source_target_pairs={{0,16},{8,24},{16,0},{24,8},{32,48},{40,56},{48,32},{56,40},{64,80... | collective-permute-start | bytes 4128776 | tf_op jit(solution)/shard_map/ppermute | solution.py:82
  499.9 34.3 %collective-permute-start.55 = (bf16[128,5376]{1,0:T(8,128)(2,1)}, bf16[128,5376]{1,0:T(8,128)(2,1)}, u32[]{:S(2)}, u32[]{:S(2)}) collective-permute-start(bf16[128,5376]{1,0:T(8,128)(2,1)} %get-tuple-element.369), channel_id=1, source_target_pairs={{0,48},{8,56},{16,32},{24,40},{32,16},{40,24},{48,0},{56,8},{64,11... | collective-permute-start | bytes 4128776 | tf_op jit(solution)/shard_map/ppermute | solution.py:82
  555.4 29.5 %collective-permute-start.61 = (bf16[128,2688]{1,0:T(8,128)(2,1)}, bf16[128,2688]{1,0:T(8,128)(2,1)S(1)}, u32[]{:S(2)}, u32[]{:S(2)}) collective-permute-start(bf16[128,2688]{1,0:T(8,128)(2,1)} %slice.162), channel_id=1, source_target_pairs={{0,64},{8,72},{16,80},{24,88},{32,96},{40,104},{48,112},{56,120},{... | collective-permute-start | bytes 2064392 | tf_op jit(solution)/shard_map/ppermute | solution.py:82
  560.3 44.6 %all-to-all-start.11 = ((bf16[128,36,128]{2,1,0:T(8,128)(2,1)}), bf16[128,36,128]{2,1,0:T(8,128)(2,1)}, u32[]{:S(2)}, u32[]{:S(2)}) async-start(bf16[128,36,128]{2,1,0:T(8,128)(2,1)} %broadcast_in_dim.62), calls=%async_computation.11 | async-start | bytes 2621440 | tf_op jit(solution)/shard_map/all_to_all | solution.py:73
  (103 other events, 1388.7 us)
